TPU v7x, 32 devices: a whole 2x2x4 slice. The times are simulated.
32 devices in a mesh: dp: 2 (over core), lon: 4 (over y, x), lat: 4 (over z).
Axes of the slice: x: 2, y: 2, z: 4, core: 2. Of those that a mesh axis runs over, the one named last changes fastest.
Arguments:
- frames: bfloat16 [4, 92, 180, 768], P('dp', 'lat', 'lon'), may hold values from -6 to 6
- regions: int32 [4, 4], P('dp'), may hold values from 0 to 180, as said below
- cotangent: bfloat16 [4, 92, 180, 768], P('dp', 'lat', 'lon'), may hold values from -6 to 6
- first_gain: bfloat16 [768], replicated, may hold values from 0.5 to 1.5
- first_shift: bfloat16 [768], replicated, may hold values from -1.75 to 1.75
- inner_weight: bfloat16 [8, 2, 96, 96], replicated, may hold values from -0.4375 to 0.4375
- inner_bias: bfloat16 [8, 2, 96], replicated, may hold values from -1.75 to 1.75
- outer_weight: bfloat16 [8, 2, 96, 96], replicated, may hold values from -0.4375 to 0.4375
- outer_bias: bfloat16 [8, 2, 96], replicated, may hold values from -1.75 to 1.75
- second_gain: bfloat16 [768], replicated, may hold values from 0.5 to 1.5
- second_shift: bfloat16 [768], replicated, may hold values from -1.75 to 1.75
- hidden_weight: bfloat16 [3072, 768], P(('dp', 'lon', 'lat')), may hold values from -0.21875 to 0.21875
- hidden_bias: bfloat16 [3072], P(('dp', 'lon', 'lat')), may hold values from -1.75 to 1.75
- output_weight: bfloat16 [3072, 768], P(('dp', 'lon', 'lat')), may hold values from -0.109375 to 0.109375
- output_bias: bfloat16 [768], replicated, may hold values from -1.75 to 1.75
Outputs:
- mixed_frames: bfloat16 [4, 92, 180, 768], P('dp', 'lat', 'lon')
- frame_grad: bfloat16 [4, 92, 180, 768], P('dp', 'lat', 'lon')
- first_gain_grad: float32 [768], replicated
- first_shift_grad: float32 [768], replicated
- inner_weight_grad: float32 [8, 2, 96, 96], replicated
- inner_bias_grad: float32 [8, 2, 96], replicated
- outer_weight_grad: float32 [8, 2, 96, 96], replicated
- outer_bias_grad: float32 [8, 2, 96], replicated
- second_gain_grad: float32 [768], replicated
- second_shift_grad: float32 [768], replicated
- hidden_weight_grad: float32 [3072, 768], P(('dp', 'lon', 'lat'))
- hidden_bias_grad: float32 [3072], P(('dp', 'lon', 'lat'))
- output_weight_grad: float32 [3072, 768], P(('dp', 'lon', 'lat'))
- output_bias_grad: float32 [768], replicated
Inputs may be any that keep to these rules, and one draw needn't show every extreme that they name: `regions`: row n is (latitude start, latitude count, longitude start, longitude count); latitude start + latitude count <= 90, latitude count at least 45, longitude count from 90 to 180, the longitude band wraps around; one frame covers the whole grid of 90 x 180.
All inputs are finite; a program needn't handle non-finite values.
Results may differ from a plain program's by a relative error of at most 0.019.
The roundings to bfloat16 on the way count: a program that leaves them out, or rounds other values in their place, can miss the bound.
Values may be sent and summed in bfloat16 or wider, within the bound.
No kernel may reach another device: no remote copies, remote signals or barrier semaphores. Data moves between devices by JAX's collectives and lax.ppermute only.
A program may use at most 320 MiB of HBM per device.

v0:
```python
import math

import jax
import jax.numpy as jnp
from jax import lax
from jax.sharding import PartitionSpec as P

H = 90


epsilon = 1e-05
shrink_level = 0.01


def tables(count, total):
    index = jnp.arange(total, dtype=jnp.int32)
    turns = index[:, None] * index[None, :] % count
    angle = turns.astype(jnp.float32) * (2.0 * math.pi / count)
    valid = (index < count).astype(jnp.float32)
    keep = valid[:, None] * valid[None, :]
    return (
        jnp.cos(angle).astype(jnp.bfloat16) * keep.astype(jnp.bfloat16),
        jnp.sin(angle).astype(jnp.bfloat16) * keep.astype(jnp.bfloat16),
    )


def layer_norm(values, gain, shift):
    centre = jnp.mean(values, axis=-1, keepdims=True)
    centred = values - centre
    spread = jnp.mean(centred * centred, axis=-1, keepdims=True)
    return centred * lax.rsqrt(spread + epsilon) * gain + shift


def smooth_gelu(values):
    return jax.nn.gelu(values, approximate=False)


def shrink(values):
    return values - shrink_level * values * lax.rsqrt(values * values + shrink_level * shrink_level)


def block_einsum(form, left, right):
    return jnp.einsum(form, left, right, preferred_element_type=jnp.float32)


def complex_mix(real, imag, weight):
    out_real = block_einsum("hkbi,bio->hkbo", real, weight[:, 0]) - block_einsum(
        "hkbi,bio->hkbo", imag, weight[:, 1]
    )
    out_imag = block_einsum("hkbi,bio->hkbo", imag, weight[:, 0]) + block_einsum(
        "hkbi,bio->hkbo", real, weight[:, 1]
    )
    return (out_real, out_imag)


def complex_back(grad_real, grad_imag, weight):
    in_real = block_einsum("hkbo,bio->hkbi", grad_real, weight[:, 0]) + block_einsum(
        "hkbo,bio->hkbi", grad_imag, weight[:, 1]
    )
    in_imag = block_einsum("hkbo,bio->hkbi", grad_imag, weight[:, 0]) - block_einsum(
        "hkbo,bio->hkbi", grad_real, weight[:, 1]
    )
    return (in_real, in_imag)


def complex_grad(real, imag, grad_real, grad_imag):
    part_real = block_einsum("hkbi,hkbo->bio", real, grad_real) + block_einsum(
        "hkbi,hkbo->bio", imag, grad_imag
    )
    part_imag = block_einsum("hkbi,hkbo->bio", real, grad_imag) - block_einsum(
        "hkbi,hkbo->bio", imag, grad_real
    )
    return jnp.stack([part_real, part_imag], axis=1)


def bias_grad(grad_real, grad_imag):
    return jnp.stack(
        [
            jnp.sum(grad_real.astype(jnp.float32), axis=(0, 1)),
            jnp.sum(grad_imag.astype(jnp.float32), axis=(0, 1)),
        ],
        axis=1,
    )


def body(
    frames,
    regions,
    cotangent,
    first_gain,
    first_shift,
    inner_weight,
    inner_bias,
    outer_weight,
    outer_bias,
    second_gain,
    second_shift,
    hidden_weight,
    hidden_bias,
    output_weight,
    output_bias,
):
    lat_count = lax.axis_size("lat")
    lon_count = lax.axis_size("lon")
    lat_place = lax.axis_index("lat")
    lon_place = lax.axis_index("lon")
    micro_count, row_count, col_count, channels = frames.shape
    height = row_count * lat_count
    breadth = col_count * lon_count
    band_width = channels // lat_count
    block_size = inner_weight.shape[2]
    owned_blocks = band_width // block_size
    first_block = lat_place * owned_blocks
    norm_scale = float(H * breadth) ** (-0.5)
    hidden_total = hidden_weight.shape[0] * lax.axis_size("dp") * lon_count * lat_count
    token_count = row_count * col_count
    cos_lon, sin_lon = tables(breadth, breadth)
    own_cos = lax.dynamic_slice_in_dim(cos_lon, lon_place * col_count, col_count, 1)
    own_sin = lax.dynamic_slice_in_dim(sin_lon, lon_place * col_count, col_count, 1)
    cos_lat, sin_lat = tables(H, height)
    inner_local = lax.dynamic_slice_in_dim(inner_weight, first_block, owned_blocks, 0)
    inner_shift = lax.dynamic_slice_in_dim(inner_bias, first_block, owned_blocks, 0).astype(
        jnp.float32
    )
    outer_local = lax.dynamic_slice_in_dim(outer_weight, first_block, owned_blocks, 0)
    outer_shift = lax.dynamic_slice_in_dim(outer_bias, first_block, owned_blocks, 0).astype(
        jnp.float32
    )
    gain_one = first_gain.astype(jnp.float32)
    shift_one = first_shift.astype(jnp.float32)
    gain_two = second_gain.astype(jnp.float32)
    shift_two = second_shift.astype(jnp.float32)
    final_shift = output_bias.astype(jnp.float32)
    lat_global = lat_place * row_count + jnp.arange(row_count, dtype=jnp.int32)
    lon_global = lon_place * col_count + jnp.arange(col_count, dtype=jnp.int32)
    field_zero = jnp.zeros((row_count, col_count, channels), jnp.float32)

    def lon_forward(running, shard_piece):
        return (
            jnp.einsum("hwc,wk->hkc", shard_piece, own_cos, preferred_element_type=jnp.float32),
            running[1]
            - jnp.einsum("hwc,wk->hkc", shard_piece, own_sin, preferred_element_type=jnp.float32),
        )

    def lon_inverse(pieces):
        return jnp.einsum(
            "hkc,kw->hwc", pieces[0], own_cos, preferred_element_type=jnp.float32
        ) - jnp.einsum("hkc,kw->hwc", pieces[1], own_sin, preferred_element_type=jnp.float32)

    def lat_forward(real, imag):
        out_real = norm_scale * (
            jnp.einsum("qh,hkc->qkc", cos_lat, real, preferred_element_type=jnp.float32)
            + jnp.einsum("qh,hkc->qkc", sin_lat, imag, preferred_element_type=jnp.float32)
        )
        out_imag = norm_scale * (
            jnp.einsum("qh,hkc->qkc", cos_lat, imag, preferred_element_type=jnp.float32)
            - jnp.einsum("qh,hkc->qkc", sin_lat, real, preferred_element_type=jnp.float32)
        )
        return (out_real, out_imag)

    def lat_inverse(real, imag):
        out_real = norm_scale * (
            jnp.einsum("hq,qkc->hkc", cos_lat, real, preferred_element_type=jnp.float32)
            - jnp.einsum("hq,qkc->hkc", sin_lat, imag, preferred_element_type=jnp.float32)
        )
        out_imag = norm_scale * (
            jnp.einsum("hq,qkc->hkc", cos_lat, imag, preferred_element_type=jnp.float32)
            + jnp.einsum("hq,qkc->hkc", sin_lat, real, preferred_element_type=jnp.float32)
        )
        return (out_real, out_imag)

    def to_blocks(values):
        return values.astype(jnp.bfloat16).reshape(height, col_count, owned_blocks, block_size)

    def step(totals, inputs):
        one_frame, region, cot_frame = inputs
        lat_in = (lat_global >= region[0]) & (lat_global < region[0] + region[1])
        lon_in = (lon_global - region[2]) % breadth < region[3]
        inside_mask = (lat_in[:, None] & lon_in[None, :]).astype(jnp.float32)[:, :, None]
        inside = one_frame.astype(jnp.float32) * inside_mask
        normed, norm_one_back = jax.vjp(layer_norm, inside, gain_one, shift_one)
        lon_real, lon_imag = lon_forward(
            (field_zero, field_zero),
            lax.all_gather(normed.astype(jnp.bfloat16), "lon", axis=1, tiled=True),
        )
        col_real, col_imag = (
            lax.all_to_all(
                lon_real.astype(jnp.bfloat16), "lat", split_axis=2, concat_axis=0, tiled=True
            ),
            lax.all_to_all(
                lon_imag.astype(jnp.bfloat16), "lat", split_axis=2, concat_axis=0, tiled=True
            ),
        )
        freq_real, freq_imag = lat_forward(col_real, col_imag)
        freq_real = to_blocks(freq_real)
        freq_imag = to_blocks(freq_imag)
        pre_real, pre_imag = complex_mix(freq_real, freq_imag, inner_local)
        hid_real, gelu_back_real = jax.vjp(smooth_gelu, pre_real + inner_shift[:, 0])
        hid_imag, gelu_back_imag = jax.vjp(smooth_gelu, pre_imag + inner_shift[:, 1])
        hid_real = hid_real.astype(jnp.bfloat16)
        hid_imag = hid_imag.astype(jnp.bfloat16)
        out_real, out_imag = complex_mix(hid_real, hid_imag, outer_local)
        spec_real, shrink_back_real = jax.vjp(shrink, out_real + outer_shift[:, 0])
        spec_imag, shrink_back_imag = jax.vjp(shrink, out_imag + outer_shift[:, 1])
        spec_real = spec_real.astype(jnp.bfloat16).reshape(height, col_count, band_width)
        spec_imag = spec_imag.astype(jnp.bfloat16).reshape(height, col_count, band_width)
        back_real, back_imag = lat_inverse(spec_real, spec_imag)
        row_real, row_imag = (
            lax.all_to_all(
                back_real.astype(jnp.bfloat16), "lat", split_axis=0, concat_axis=2, tiled=True
            ),
            lax.all_to_all(
                back_imag.astype(jnp.bfloat16), "lat", split_axis=0, concat_axis=2, tiled=True
            ),
        )
        filtered = lon_inverse(
            (
                lax.all_gather(row_real, "lon", axis=1, tiled=True),
                lax.all_gather(row_imag, "lon", axis=1, tiled=True),
            )
        )
        mixed_field = filtered + normed + inside
        second, norm_two_back = jax.vjp(layer_norm, mixed_field, gain_two, shift_two)
        tokens = second.astype(jnp.bfloat16).reshape(token_count, channels)
        preact = jnp.einsum(
            "tc,fc->tf",
            tokens,
            lax.all_gather(hidden_weight, ("dp", "lon", "lat"), axis=0, tiled=True),
            preferred_element_type=jnp.float32,
        ) + lax.all_gather(hidden_bias, ("dp", "lon", "lat"), axis=0, tiled=True).astype(
            jnp.float32
        )
        hidden_act = smooth_gelu(preact).astype(jnp.bfloat16)
        branch = jnp.einsum(
            "tf,fc->tc",
            hidden_act,
            lax.all_gather(output_weight, ("dp", "lon", "lat"), axis=0, tiled=True),
            preferred_element_type=jnp.float32,
        )
        weights_now = (
            lax.all_gather(hidden_weight, ("dp", "lon", "lat"), axis=0, tiled=True),
            lax.all_gather(hidden_bias, ("dp", "lon", "lat"), axis=0, tiled=True),
            lax.all_gather(output_weight, ("dp", "lon", "lat"), axis=0, tiled=True),
        )
        branch = branch.reshape(row_count, col_count, channels) + final_shift
        mixed_frame = ((mixed_field + branch) * inside_mask).astype(jnp.bfloat16)
        grad_out = cot_frame.astype(jnp.float32) * inside_mask
        grad_branch = grad_out.astype(jnp.bfloat16).reshape(token_count, channels)
        output_bias_part = jnp.sum(grad_branch.astype(jnp.float32), axis=0)
        rows_in, bias_in, rows_out = weights_now
        preact = jnp.einsum(
            "tc,fc->tf", tokens, rows_in, preferred_element_type=jnp.float32
        ) + bias_in.astype(jnp.float32)
        hidden_act, gelu_back_hidden = jax.vjp(smooth_gelu, preact)
        hidden_low = hidden_act.astype(jnp.bfloat16)
        output_weight_part = jnp.einsum(
            "tf,tc->fc", hidden_low, grad_branch, preferred_element_type=jnp.float32
        )
        grad_hidden = jnp.einsum(
            "tc,fc->tf", grad_branch, rows_out, preferred_element_type=jnp.float32
        )
        grad_preact = gelu_back_hidden(grad_hidden)[0].astype(jnp.bfloat16)
        hidden_weight_part = jnp.einsum(
            "tf,tc->fc", grad_preact, tokens, preferred_element_type=jnp.float32
        )
        hidden_bias_part = jnp.sum(grad_preact.astype(jnp.float32), axis=0)
        grad_second = jnp.einsum(
            "tf,fc->tc", grad_preact, rows_in, preferred_element_type=jnp.float32
        )
        grad_mixed_part, second_gain_part, second_shift_part = norm_two_back(
            grad_second.reshape(row_count, col_count, channels)
        )
        grad_mixed = grad_out + grad_mixed_part
        grad_rows_real, grad_rows_imag = lon_forward(
            (field_zero, field_zero),
            lax.all_gather(grad_mixed.astype(jnp.bfloat16), "lon", axis=1, tiled=True),
        )
        grad_back_real, grad_back_imag = (
            lax.all_to_all(
                grad_rows_real.astype(jnp.bfloat16), "lat", split_axis=2, concat_axis=0, tiled=True
            ),
            lax.all_to_all(
                grad_rows_imag.astype(jnp.bfloat16), "lat", split_axis=2, concat_axis=0, tiled=True
            ),
        )
        grad_spec_real, grad_spec_imag = lat_forward(grad_back_real, grad_back_imag)
        grad_spec_real = grad_spec_real.reshape(height, col_count, owned_blocks, block_size)
        grad_spec_imag = grad_spec_imag.reshape(height, col_count, owned_blocks, block_size)
        grad_out_real = shrink_back_real(grad_spec_real)[0].astype(jnp.bfloat16)
        grad_out_imag = shrink_back_imag(grad_spec_imag)[0].astype(jnp.bfloat16)
        outer_weight_part = complex_grad(hid_real, hid_imag, grad_out_real, grad_out_imag)
        outer_bias_part = bias_grad(grad_out_real, grad_out_imag)
        grad_hid_real, grad_hid_imag = complex_back(grad_out_real, grad_out_imag, outer_local)
        grad_pre_real = gelu_back_real(grad_hid_real)[0].astype(jnp.bfloat16)
        grad_pre_imag = gelu_back_imag(grad_hid_imag)[0].astype(jnp.bfloat16)
        inner_weight_part = complex_grad(freq_real, freq_imag, grad_pre_real, grad_pre_imag)
        inner_bias_part = bias_grad(grad_pre_real, grad_pre_imag)
        grad_freq_real, grad_freq_imag = complex_back(grad_pre_real, grad_pre_imag, inner_local)
        grad_freq_real = grad_freq_real.astype(jnp.bfloat16).reshape(height, col_count, band_width)
        grad_freq_imag = grad_freq_imag.astype(jnp.bfloat16).reshape(height, col_count, band_width)
        grad_col_real, grad_col_imag = lat_inverse(grad_freq_real, grad_freq_imag)
        grad_lon_real, grad_lon_imag = (
            lax.all_to_all(
                grad_col_real.astype(jnp.bfloat16), "lat", split_axis=0, concat_axis=2, tiled=True
            ),
            lax.all_to_all(
                grad_col_imag.astype(jnp.bfloat16), "lat", split_axis=0, concat_axis=2, tiled=True
            ),
        )
        grad_normed_part = lon_inverse(
            (
                lax.all_gather(grad_lon_real, "lon", axis=1, tiled=True),
                lax.all_gather(grad_lon_imag, "lon", axis=1, tiled=True),
            )
        )
        grad_normed = grad_normed_part + grad_mixed
        grad_inside_part, first_gain_part, first_shift_part = norm_one_back(grad_normed)
        frame_grad = ((grad_inside_part + grad_mixed) * inside_mask).astype(jnp.bfloat16)
        parts = (
            hidden_weight_part,
            hidden_bias_part,
            output_weight_part,
            first_gain_part,
            first_shift_part,
            inner_weight_part,
            inner_bias_part,
            outer_weight_part,
            outer_bias_part,
            second_gain_part,
            second_shift_part,
            output_bias_part,
        )
        new_totals = tuple((total + part for total, part in zip(totals, parts)))
        return (new_totals, (mixed_frame, frame_grad))

    initial = (
        jnp.zeros((hidden_total, channels), jnp.float32),
        jnp.zeros((hidden_total,), jnp.float32),
        jnp.zeros((hidden_total, channels), jnp.float32),
        jnp.zeros((channels,), jnp.float32),
        jnp.zeros((channels,), jnp.float32),
        jnp.zeros((owned_blocks, 2, block_size, block_size), jnp.float32),
        jnp.zeros((owned_blocks, 2, block_size), jnp.float32),
        jnp.zeros((owned_blocks, 2, block_size, block_size), jnp.float32),
        jnp.zeros((owned_blocks, 2, block_size), jnp.float32),
        jnp.zeros((channels,), jnp.float32),
        jnp.zeros((channels,), jnp.float32),
        jnp.zeros((channels,), jnp.float32),
    )
    totals, outputs = lax.scan(step, initial, (frames, regions, cotangent))
    mixed_frames, frame_grads = outputs
    ffn_sums = (
        lax.psum_scatter(totals[0], ("dp", "lon", "lat"), scatter_dimension=0, tiled=True),
        lax.psum_scatter(totals[1], ("dp", "lon", "lat"), scatter_dimension=0, tiled=True),
        lax.psum_scatter(totals[2], ("dp", "lon", "lat"), scatter_dimension=0, tiled=True),
    )
    inner_full = lax.dynamic_update_slice_in_dim(
        jnp.zeros(inner_weight.shape, jnp.float32), totals[5], first_block, 0
    )
    inner_bias_full = lax.dynamic_update_slice_in_dim(
        jnp.zeros(inner_bias.shape, jnp.float32), totals[6], first_block, 0
    )
    outer_full = lax.dynamic_update_slice_in_dim(
        jnp.zeros(outer_weight.shape, jnp.float32), totals[7], first_block, 0
    )
    outer_bias_full = lax.dynamic_update_slice_in_dim(
        jnp.zeros(outer_bias.shape, jnp.float32), totals[8], first_block, 0
    )
    small_sums = lax.psum(
        (
            totals[3],
            totals[4],
            inner_full,
            inner_bias_full,
            outer_full,
            outer_bias_full,
            totals[9],
            totals[10],
            totals[11],
        ),
        ("dp", "lon", "lat"),
    )
    return (
        mixed_frames,
        frame_grads,
        small_sums[0],
        small_sums[1],
        small_sums[2],
        small_sums[3],
        small_sums[4],
        small_sums[5],
        small_sums[6],
        small_sums[7],
        ffn_sums[0],
        ffn_sums[1],
        ffn_sums[2],
        small_sums[8],
    )


def solution(mesh):
    return jax.shard_map(
        body,
        mesh=mesh,
        in_specs=(
            P("dp", "lat", "lon", None),
            P("dp", None),
            P("dp", "lat", "lon", None),
            P(),
            P(),
            P(),
            P(),
            P(),
            P(),
            P(),
            P(),
            P(("dp", "lon", "lat"), None),
            P(("dp", "lon", "lat")),
            P(("dp", "lon", "lat"), None),
            P(),
        ),
        out_specs=(
            P("dp", "lat", "lon", None),
            P("dp", "lat", "lon", None),
            P(),
            P(),
            P(),
            P(),
            P(),
            P(),
            P(),
            P(),
            P(("dp", "lon", "lat"), None),
            P(("dp", "lon", "lat")),
            P(("dp", "lon", "lat"), None),
            P(),
        ),
        check_vma=False,
    )
```

profile of v0, /device:TPU:0, one launch (start us, length us, event | category | flops | bytes accessed | tf_op | source)
XLA Modules:
  0.0 2790.6 jit_solution(13805945086366492397)
XLA Ops:
  22.3 2335.3 %while.42 = (s32[]{:T(128)}, f32[3072,768]{1,0:T(8,128)}, f32[3072]{0:T(1024)}, f32[3072,768]{1,0:T(8,128)}, f32[768]{0:T(1024)}, /*index=5*/f32[768]{0:T(1024)}...) while((s32[]{:T(128)}, f32[3072,768]{1,0:T(8,128)}, ...), condition=%wide.region_19.20_spmd.clone.clone.clone.clone, body=%wide.region_0.19_spmd.clone.clone.clone.clone.sunk | while | flops 38150266880 | bytes 1333820928 | solution.py:350
  33.0 75.9 %all-gather.9.cloned.1.call-done = bf16[23,180,768]{2,0,1:T(8,128)(2,1)} async-done(((bf16[23,45,768]{2,0,1:T(8,128)(2,1)}), bf16[23,180,768]{2,0,1:T(8,128)(2,1)}) %all-gather.9.cloned.1.call-update) | async-done | bytes 6359056 | tf_op jit(solution)/shard_map/while/body/eval_jaxpr/all_gather | solution.py:184
  302.4 54.8 %all_to_all.360 = bf16[92,45,192]{2,1,0:T(8,128)(2,1)S(1)} all-to-all(bf16[92,45,192]{2,1,0:T(8,128)(2,1)} %copy.372), channel_id=1, replica_groups=mesh['dp'=2,'lon'=4,'lat'=4] {'lat'}, dimensions={0} | all-to-all | bytes 3179520 | tf_op jit(solution)/shard_map/while/body/eval_jaxpr/all_to_all | solution.py:212
  373.3 53.3 %all_to_all.361 = bf16[92,45,192]{2,1,0:T(8,128)(2,1)S(1)} all-to-all(bf16[92,45,192]{2,1,0:T(8,128)(2,1)S(1)} %copy.374), channel_id=1, replica_groups=mesh['dp'=2,'lon'=4,'lat'=4] {'lat'}, dimensions={0} | all-to-all | bytes 3179520 | tf_op jit(solution)/shard_map/while/body/eval_jaxpr/all_to_all | solution.py:209
  432.7 38.8 %all-reduce.8 = bf16[3072]{0:T(1024)(128)(2,1)S(1)} all-reduce(bf16[3072]{0:T(1024)(128)(2,1)S(1)} %dynamic-update-slice.5), channel_id=1, replica_groups=mesh['dp'=2,'lon'=4,'lat'=4] {'dp','lon','lat'}, use_global_device_ids=true, to_apply=%add | all-reduce | flops 3072 | bytes 12288 | tf_op jit(solution)/shard_map/while
  482.8 29.2 %all-gather.13.cloned.1.call-done = bf16[23,180,768]{2,0,1:T(8,128)(2,1)} async-done(((bf16[23,45,768]{2,0,1:T(8,128)(2,1)}), bf16[23,180,768]{2,0,1:T(8,128)(2,1)}) %all-gather.13.cloned.1.call-update) | async-done | bytes 6359056 | tf_op jit(solution)/shard_map/while/body/eval_jaxpr/all_gather | solution.py:218
  522.9 55.4 %all-gather.15.cloned.1.call-done = bf16[3072,768]{1,0:T(8,128)(2,1)} async-done(((bf16[96,768]{1,0:T(8,128)(2,1)}), bf16[3072,768]{1,0:T(8,128)(2,1)}) %all-gather.15.cloned.1.call-update) | async-done | bytes 4718608 | tf_op jit(solution)/shard_map/while/body/eval_jaxpr/all_gather | solution.py:241
  578.3 37.4 %multiply_convert_fusion.22 = (bf16[1035,3072]{1,0:T(8,128)(2,1)}, f32[1035,3072]{1,0:T(8,128)}, f32[1035,3072]{1,0:T(8,128)}) fusion(f32[3072]{0:T(1024)S(1)} %convert_element_type.1096, bf16[1035,768]{1,0:T(8,128)(2,1)} %reshape.370, bf16[3072,768]{1,0:T(8,128)(2,1)} %all-gather.15.cloned.1.call-done), kind=kOutput, calls=%fused_computation.7.clone.1 | convolution fusion | flops 5093591040 | bytes 38115840 | tf_op jit(solution)/shard_map/while/body/eval_jaxpr/tc,fc->tf/dot_general | solution.py:251
  685.5 72.0 %all-gather.19.cloned.1.call-done = bf16[23,180,768]{2,0,1:T(8,128)(2,1)} async-done(((bf16[23,45,768]{2,0,1:T(8,128)(2,1)}), bf16[23,180,768]{2,0,1:T(8,128)(2,1)}) %all-gather.19.cloned.1.call-update) | async-done | bytes 6359056 | tf_op jit(solution)/shard_map/while/body/eval_jaxpr/all_gather | solution.py:276
  963.9 54.8 %all_to_all.362 = bf16[92,45,192]{2,1,0:T(8,128)(2,1)S(1)} all-to-all(bf16[92,45,192]{2,1,0:T(8,128)(2,1)} %copy.389), channel_id=1, replica_groups=mesh['dp'=2,'lon'=4,'lat'=4] {'lat'}, dimensions={0} | all-to-all | bytes 3179520 | tf_op jit(solution)/shard_map/while/body/eval_jaxpr/all_to_all | solution.py:306
  1043.4 48.7 %all-to-all-done.7 = bf16[92,45,192]{2,1,0:T(8,128)(2,1)} async-done(((bf16[92,45,192]{2,1,0:T(8,128)(2,1)}), bf16[92,45,192]{2,1,0:T(8,128)(2,1)}, u32[]{:S(2)}, u32[]{:S(2)}) %all-to-all-start.7) | async-done | bytes 1589792 | tf_op jit(solution)/shard_map/while/body/eval_jaxpr/all_to_all | solution.py:303
  1199.3 73.2 %all-gather.9.cloned.1.call-done = bf16[23,180,768]{2,0,1:T(8,128)(2,1)} async-done(((bf16[23,45,768]{2,0,1:T(8,128)(2,1)}), bf16[23,180,768]{2,0,1:T(8,128)(2,1)}) %all-gather.9.cloned.1.call-update) | async-done | bytes 6359056 | tf_op jit(solution)/shard_map/while/body/eval_jaxpr/all_gather | solution.py:184
  1465.9 54.8 %all_to_all.360 = bf16[92,45,192]{2,1,0:T(8,128)(2,1)S(1)} all-to-all(bf16[92,45,192]{2,1,0:T(8,128)(2,1)} %copy.372), channel_id=1, replica_groups=mesh['dp'=2,'lon'=4,'lat'=4] {'lat'}, dimensions={0} | all-to-all | bytes 3179520 | tf_op jit(solution)/shard_map/while/body/eval_jaxpr/all_to_all | solution.py:212
  1536.8 53.3 %all_to_all.361 = bf16[92,45,192]{2,1,0:T(8,128)(2,1)S(1)} all-to-all(bf16[92,45,192]{2,1,0:T(8,128)(2,1)S(1)} %copy.374), channel_id=1, replica_groups=mesh['dp'=2,'lon'=4,'lat'=4] {'lat'}, dimensions={0} | all-to-all | bytes 3179520 | tf_op jit(solution)/shard_map/while/body/eval_jaxpr/all_to_all | solution.py:209
  1596.4 38.8 %all-reduce.8 = bf16[3072]{0:T(1024)(128)(2,1)S(1)} all-reduce(bf16[3072]{0:T(1024)(128)(2,1)S(1)} %dynamic-update-slice.5), channel_id=1, replica_groups=mesh['dp'=2,'lon'=4,'lat'=4] {'dp','lon','lat'}, use_global_device_ids=true, to_apply=%add | all-reduce | flops 3072 | bytes 12288 | tf_op jit(solution)/shard_map/while
  1686.4 55.3 %all-gather.15.cloned.1.call-done = bf16[3072,768]{1,0:T(8,128)(2,1)} async-done(((bf16[96,768]{1,0:T(8,128)(2,1)}), bf16[3072,768]{1,0:T(8,128)(2,1)}) %all-gather.15.cloned.1.call-update) | async-done | bytes 4718608 | tf_op jit(solution)/shard_map/while/body/eval_jaxpr/all_gather | solution.py:241
  1741.8 37.4 %multiply_convert_fusion.22 = (bf16[1035,3072]{1,0:T(8,128)(2,1)}, f32[1035,3072]{1,0:T(8,128)}, f32[1035,3072]{1,0:T(8,128)}) fusion(f32[3072]{0:T(1024)S(1)} %convert_element_type.1096, bf16[1035,768]{1,0:T(8,128)(2,1)} %reshape.370, bf16[3072,768]{1,0:T(8,128)(2,1)} %all-gather.15.cloned.1.call-done), kind=kOutput, calls=%fused_computation.7.clone.1 | convolution fusion | flops 5093591040 | bytes 38115840 | tf_op jit(solution)/shard_map/while/body/eval_jaxpr/tc,fc->tf/dot_general | solution.py:251
  1849.2 72.0 %all-gather.19.cloned.1.call-done = bf16[23,180,768]{2,0,1:T(8,128)(2,1)} async-done(((bf16[23,45,768]{2,0,1:T(8,128)(2,1)}), bf16[23,180,768]{2,0,1:T(8,128)(2,1)}) %all-gather.19.cloned.1.call-update) | async-done | bytes 6359056 | tf_op jit(solution)/shard_map/while/body/eval_jaxpr/all_gather | solution.py:276
  2127.6 54.8 %all_to_all.362 = bf16[92,45,192]{2,1,0:T(8,128)(2,1)S(1)} all-to-all(bf16[92,45,192]{2,1,0:T(8,128)(2,1)} %copy.389), channel_id=1, replica_groups=mesh['dp'=2,'lon'=4,'lat'=4] {'lat'}, dimensions={0} | all-to-all | bytes 3179520 | tf_op jit(solution)/shard_map/while/body/eval_jaxpr/all_to_all | solution.py:306
  2207.1 48.7 %all-to-all-done.7 = bf16[92,45,192]{2,1,0:T(8,128)(2,1)} async-done(((bf16[92,45,192]{2,1,0:T(8,128)(2,1)}), bf16[92,45,192]{2,1,0:T(8,128)(2,1)}, u32[]{:S(2)}, u32[]{:S(2)}) %all-to-all-start.7) | async-done | bytes 1589792 | tf_op jit(solution)/shard_map/while/body/eval_jaxpr/all_to_all | solution.py:303
  2371.9 40.9 %all-reduce.5 = (f32[768]{0:T(1024)}, f32[768]{0:T(1024)}, f32[8,2,96]{2,1,0:T(2,128)}, f32[8,2,96]{2,1,0:T(2,128)}, f32[768]{0:T(1024)}, /*index=5*/f32[768]{0:T(1024)}, f32[3072]{0:T(1024)S(1)}, f32[768]{0:T(1024)}) all-reduce(f32[768]{0:T(1024)S(1)} %copy-done.87, ...), channel_id=1, replica_groups=mesh['dp'=2,'lon'=4,'lat'=4] {'dp','lon','lat'}, use_global_device_ids=true, to_apply=%region_20.21 | all-reduce | flops 9984 | bytes 79872 | tf_op jit(solution)/shard_map/psum | solution.py:369
  2413.4 82.7 %all-reduce.11.cloned.1.call-done = (f32[8,2,96,96]{3,2,1,0:T(8,128)}, f32[8,2,96,96]{3,2,1,0:T(8,128)}) async-done(((f32[8,2,96,96]{3,2,1,0:T(8,128)}, f32[8,2,96,96]{3,2,1,0:T(8,128)}), (f32[8,2,96,96]{3,2,1,0:T(8,128)}, f32[8,2,96,96]{3,2,1,0:T(8,128)})) %all-reduce.11.cloned.1.call-update) | async-done | bytes 1179664 | tf_op jit(solution)/shard_map/psum | solution.py:369
  2496.1 140.8 %reduce-scatter.3.cloned.1.call-done = f32[96,768]{1,0:T(8,128)} async-done(((f32[3072,768]{1,0:T(8,128)}), f32[96,768]{1,0:T(8,128)}) %reduce-scatter.3.cloned.1.call-update) | async-done | bytes 294928 | tf_op jit(solution)/shard_map/reduce_scatter | solution.py:353
  2637.0 141.9 %reduce-scatter.5.cloned.1.call-done = f32[96,768]{1,0:T(8,128)} async-done(((f32[3072,768]{1,0:T(8,128)}), f32[96,768]{1,0:T(8,128)}) %reduce-scatter.5.cloned.1.call-update) | async-done | bytes 294928 | tf_op jit(solution)/shard_map/reduce_scatter | solution.py:355
  (839 shorter events, 1348.1 us)
Async XLA Ops:
  22.3 86.6 %all-gather.9.cloned.1.call-start = ((), (), s32[]{:S(2)}) async-start(), calls=%async_computation.13 | async-start | bytes 8294400 | tf_op jit(solution)/shard_map/while/body/eval_jaxpr/all_gather | solution.py:184
  173.7 302.8 %all-gather.11.cloned.1.call-start = ((), (), s32[]{:S(2)}) async-start(), calls=%async_computation.14 | async-start | bytes 8294400 | tf_op jit(solution)/shard_map/while/body/eval_jaxpr/all_gather | solution.py:219
  364.7 147.3 %all-gather.13.cloned.1.call-start = ((), (), s32[]{:S(2)}) async-start(), calls=%async_computation.15 | async-start | bytes 8294400 | tf_op jit(solution)/shard_map/while/body/eval_jaxpr/all_gather | solution.py:218
  431.2 147.1 %all-gather.15.cloned.1.call-start = ((), (), s32[]{:S(2)}) async-start(), calls=%async_computation.16 | async-start | bytes 4866048 | tf_op jit(solution)/shard_map/while/body/eval_jaxpr/all_gather | solution.py:241
  431.8 211.6 %all-gather.17.cloned.1.call-start = ((), (), s32[]{:S(2)}) async-start(), calls=%async_computation.17 | async-start | bytes 4866048 | tf_op jit(solution)/shard_map/while/body/eval_jaxpr/all_gather | solution.py:243
  432.3 325.1 %all-gather.19.cloned.1.call-start = ((), (), s32[]{:S(2)}) async-start(), calls=%async_computation.18 | async-start | bytes 8294400 | tf_op jit(solution)/shard_map/while/body/eval_jaxpr/all_gather | solution.py:276
  776.0 42.3 %all-to-all-start.5 = ((bf16[4,2,99360]{2,1,0:T(2,128)(2,1)}), bf16[4,2,99360]{2,1,0:T(2,128)(2,1)S(1)}, u32[]{:S(2)}, u32[]{:S(2)}) async-start(bf16[4,2,99360]{2,1,0:T(2,128)(2,1)} %reshape.375), calls=%async_computation.5 | async-start | bytes 3182592 | tf_op jit(solution)/shard_map/while/body/eval_jaxpr/all_to_all | solution.py:279
  822.7 325.4 %all-gather.21.cloned.1.call-start = ((), (), s32[]{:S(2)}) async-start(), calls=%async_computation.19 | async-start | bytes 8294400 | tf_op jit(solution)/shard_map/while/body/eval_jaxpr/all_gather | solution.py:313
  1036.9 55.2 %all-to-all-start.7 = ((bf16[92,45,192]{2,1,0:T(8,128)(2,1)}), bf16[92,45,192]{2,1,0:T(8,128)(2,1)}, u32[]{:S(2)}, u32[]{:S(2)}) async-start(bf16[92,45,192]{2,1,0:T(8,128)(2,1)} %copy.391), calls=%async_computation.7 | async-start | bytes 4521984 | tf_op jit(solution)/shard_map/while/body/eval_jaxpr/all_to_all | solution.py:303
  1041.4 131.5 %all-gather.23.cloned.1.call-start = ((), (), s32[]{:S(2)}) async-start(), calls=%async_computation.20 | async-start | bytes 8294400 | tf_op jit(solution)/shard_map/while/body/eval_jaxpr/all_gather | solution.py:312
  1188.6 83.9 %all-gather.9.cloned.1.call-start = ((), (), s32[]{:S(2)}) async-start(), calls=%async_computation.13 | async-start | bytes 8294400 | tf_op jit(solution)/shard_map/while/body/eval_jaxpr/all_gather | solution.py:184
  1291.0 42.0 %all-to-all-start.1 = ((bf16[4,2,99360]{2,1,0:T(2,128)(2,1)}), bf16[4,2,99360]{2,1,0:T(2,128)(2,1)S(1)}, u32[]{:S(2)}, u32[]{:S(2)}) async-start(bf16[4,2,99360]{2,1,0:T(2,128)(2,1)} %reshape.368), calls=%async_computation.1 | async-start | bytes 3182592 | tf_op jit(solution)/shard_map/while/body/eval_jaxpr/all_to_all | solution.py:187
  1337.3 302.9 %all-gather.11.cloned.1.call-start = ((), (), s32[]{:S(2)}) async-start(), calls=%async_computation.14 | async-start | bytes 8294400 | tf_op jit(solution)/shard_map/while/body/eval_jaxpr/all_gather | solution.py:219
  1528.2 147.3 %all-gather.13.cloned.1.call-start = ((), (), s32[]{:S(2)}) async-start(), calls=%async_computation.15 | async-start | bytes 8294400 | tf_op jit(solution)/shard_map/while/body/eval_jaxpr/all_gather | solution.py:218
  1594.7 147.0 %all-gather.15.cloned.1.call-start = ((), (), s32[]{:S(2)}) async-start(), calls=%async_computation.16 | async-start | bytes 4866048 | tf_op jit(solution)/shard_map/while/body/eval_jaxpr/all_gather | solution.py:241
  1595.3 211.7 %all-gather.17.cloned.1.call-start = ((), (), s32[]{:S(2)}) async-start(), calls=%async_computation.17 | async-start | bytes 4866048 | tf_op jit(solution)/shard_map/while/body/eval_jaxpr/all_gather | solution.py:243
  1596.1 325.1 %all-gather.19.cloned.1.call-start = ((), (), s32[]{:S(2)}) async-start(), calls=%async_computation.18 | async-start | bytes 8294400 | tf_op jit(solution)/shard_map/while/body/eval_jaxpr/all_gather | solution.py:276
  1939.7 42.3 %all-to-all-start.5 = ((bf16[4,2,99360]{2,1,0:T(2,128)(2,1)}), bf16[4,2,99360]{2,1,0:T(2,128)(2,1)S(1)}, u32[]{:S(2)}, u32[]{:S(2)}) async-start(bf16[4,2,99360]{2,1,0:T(2,128)(2,1)} %reshape.375), calls=%async_computation.5 | async-start | bytes 3182592 | tf_op jit(solution)/shard_map/while/body/eval_jaxpr/all_to_all | solution.py:279
  1986.4 329.2 %all-gather.21.cloned.1.call-start = ((), (), s32[]{:S(2)}) async-start(), calls=%async_computation.19 | async-start | bytes 8294400 | tf_op jit(solution)/shard_map/while/body/eval_jaxpr/all_gather | solution.py:313
  2200.6 55.2 %all-to-all-start.7 = ((bf16[92,45,192]{2,1,0:T(8,128)(2,1)}), bf16[92,45,192]{2,1,0:T(8,128)(2,1)}, u32[]{:S(2)}, u32[]{:S(2)}) async-start(bf16[92,45,192]{2,1,0:T(8,128)(2,1)} %copy.391), calls=%async_computation.7 | async-start | bytes 4521984 | tf_op jit(solution)/shard_map/while/body/eval_jaxpr/all_to_all | solution.py:303
  2205.1 131.5 %all-gather.23.cloned.1.call-start = ((), (), s32[]{:S(2)}) async-start(), calls=%async_computation.20 | async-start | bytes 8294400 | tf_op jit(solution)/shard_map/while/body/eval_jaxpr/all_gather | solution.py:312
  2357.6 138.5 %all-reduce.11.cloned.1.call-start = ((), (), s32[]{:S(2)}) async-start(), calls=%async_computation.12 | async-start | bytes 3145728 | tf_op jit(solution)/shard_map/psum | solution.py:369
  2360.9 276.1 %reduce-scatter.3.cloned.1.call-start = ((), (), s32[]{:S(2)}) async-start(), calls=%async_computation.10 | async-start | bytes 9732096 | tf_op jit(solution)/shard_map/reduce_scatter | solution.py:353
  2361.5 417.4 %reduce-scatter.5.cloned.1.call-start = ((), (), s32[]{:S(2)}) async-start(), calls=%async_computation.11 | async-start | bytes 9732096 | tf_op jit(solution)/shard_map/reduce_scatter | solution.py:355
  (223 other events, 7540.2 us)
Sparse Core Ops, SparseCore 0:
  33.2 75.7 all-gather.8
  364.8 71.1 all-gather.10
  438.4 73.5 all-gather.12
  514.7 63.5 all-gather.14
  580.9 62.3 all-gather.16
  685.6 71.8 all-gather.18
  1026.3 71.1 all-gather.20
  1101.7 71.1 all-gather.22
  1199.4 73.0 all-gather.8
  1528.4 71.1 all-gather.10
  1602.0 73.4 all-gather.12
  1678.2 63.5 all-gather.14
  1744.6 62.3 all-gather.16
  1849.3 71.8 all-gather.18
  2190.0 71.1 all-gather.20
  2265.4 71.1 all-gather.22
Sparse Core Ops, SparseCore 1:
  2364.1 131.9 all-reduce.10
  2502.5 134.4 reduce-scatter.2
  2644.3 134.5 reduce-scatter.4
where the time goes:
time: 2800 us; the launch traced here: 2790 us
  waiting for transfers between devices  1140 us (41%)
  local copies, waits for them, and re-layouts  549 us (20%)
  matrix products  511 us (18%)
  blocking collectives  444 us (16%)
  other arithmetic  73.8 us (3%)
  starting transfers between devices  47.3 us (2%)
    while x420, local copies, waits for them, and re-layouts  169 us
    all_gather x2, waiting for transfers between devices, step(): lax.all_gather(normed.astype(jnp.bfloat16), 'lon', axis=1, tiled=True)  149 us
    all_gather x2, waiting for transfers between devices, step(): lax.all_gather(grad_mixed.astype(jnp.bfloat16), 'lon', axis=1, tiled=True)  144 us
    dot_general x48, matrix products, block_einsum(): return jnp.einsum(form, left, right, preferred_element_type=jnp.float32)  142 us
    reduce_scatter x1, waiting for transfers between devices, body(): lax.psum_scatter(totals[2], ('dp', 'lon', 'lat'), scatter_dimension=0, ti...  142 us
    reduce_scatter x1, waiting for transfers between devices, body(): lax.psum_scatter(totals[0], ('dp', 'lon', 'lat'), scatter_dimension=0, ti...  141 us
    all_gather x2, waiting for transfers between devices, step(): lax.all_gather(hidden_weight, ('dp', 'lon', 'lat'), axis=0, tiled=True)  111 us
    all_to_all x2, blocking collectives, step(): lax.all_to_all(grad_col_imag.astype(jnp.bfloat16), 'lat', split_axis=0, c...  110 us
  transfers between devices with their start and end apart: 29, of which 25 were waited for; matrix products, arithmetic and copies ran while one was open for 16% of the time, Pallas kernels for 0%

commit v1 on v0

v1 whole, which is shorter than its diff:
```python
import functools
import math

import jax
import jax.numpy as jnp
import numpy as np
from jax import lax
from jax.experimental import pallas as pl
from jax.experimental.pallas import tpu as pltpu
from jax.sharding import PartitionSpec as P

H = 90
LANES = 128
GROUP = 4
KSTEP = 4

epsilon = 1e-05
shrink_level = 0.01

f32 = jnp.float32
bf16 = jnp.bfloat16


class Plan:
    def __init__(self, micro, rows, cols, channels, blocks, lat, lon):
        self.micro, self.rows, self.cols, self.channels, self.blocks = micro, rows, cols, channels, blocks
        self.lat, self.lon = lat, lon
        self.size = channels // blocks
        self.groups = -(-rows // GROUP)
        self.used = self.groups * cols
        self.packed = -(-self.used // 16) * 16
        self.padcol = -(-cols // 16) * 16
        self.stage = self.groups * self.padcol
        self.window = -(-(cols + 15) // 16) * 16
        self.slots = lat * self.groups * GROUP
        self.height = rows * lat
        self.breadth = cols * lon
        self.lanes = GROUP * self.size
        self.scale = float(H * self.breadth) ** (-0.5)

    def window_start(self, g):
        return min(self.cols * g // 16 * 16, self.packed - self.window)


def angle_tables(count, total):
    index = np.arange(total)
    turns = (index[:, None] * index[None, :]) % count
    angle = turns * (2.0 * math.pi / count)
    keep = ((index[:, None] < count) & (index[None, :] < count)).astype(np.float64)
    return np.cos(angle) * keep, np.sin(angle) * keep


def lon_tables(plan):
    cos, sin = angle_tables(plan.breadth, plan.breadth)
    breadth, win = plan.breadth, plan.window
    out = np.zeros((plan.groups, 2 * breadth, plan.lon * win), np.float32)
    for g in range(plan.groups):
        offset = plan.cols * g - plan.window_start(g)
        for s in range(plan.lon):
            w = slice(s * plan.cols, (s + 1) * plan.cols)
            at = slice(s * win + offset, s * win + offset + plan.cols)
            out[g, :breadth, at] = cos[:, w]
            out[g, breadth:, at] = -sin[:, w]
    return out.astype(jnp.bfloat16), np.ascontiguousarray(out.transpose(0, 2, 1)).astype(jnp.bfloat16)


def lat_tables(plan):
    cos, sin = angle_tables(H, plan.height)
    n = plan.slots
    slot = np.array(
        [s * plan.groups * GROUP + r for s in range(plan.lat) for r in range(plan.rows)]
    )
    c = np.zeros((n, n))
    s = np.zeros((n, n))
    c[: plan.height, slot] = cos
    s[: plan.height, slot] = sin
    forward = np.block([[c, s], [-s, c]])
    inverse = np.block([[c.T, -s.T], [s.T, c.T]])
    return forward.astype(np.float32).astype(jnp.bfloat16), inverse.astype(np.float32).astype(jnp.bfloat16)


def pack_table(plan):
    out = np.zeros((plan.packed, plan.stage), np.float32)
    for g in range(plan.groups):
        for j in range(plan.cols):
            out[plan.cols * g + j, plan.padcol * g + j] = 1.0
    return out.astype(jnp.bfloat16), np.ascontiguousarray(out.T).astype(jnp.bfloat16)


def dot(a, b):
    return lax.dot_general(a, b, (((1,), (0,)), ((), ())), preferred_element_type=f32)


def dot_nt(a, b):
    return lax.dot_general(a, b, (((1,), (1,)), ((), ())), preferred_element_type=f32)


def dot_tn(a, b):
    return lax.dot_general(a, b, (((0,), (0,)), ((), ())), preferred_element_type=f32)


def gelu_pair(x):
    phi = 0.5 + 0.5 * lax.erf(x * (0.5**0.5))
    density = jnp.exp(-0.5 * x * x) * (1.0 / math.sqrt(2.0 * math.pi))
    return x * phi, phi + x * density


def full(shape):
    return pl.BlockSpec(shape, lambda *_: (0,) * len(shape), pipeline_mode=pl.Buffered(1))


def params(mib):
    return pltpu.CompilerParams(vmem_limit_bytes=mib * 2**20)


def token_mask(plan, meta_ref, frame, i):
    p = lax.broadcasted_iota(jnp.int32, (plan.packed, 1), 0)
    g = jnp.zeros_like(p)
    for t in range(1, plan.groups):
        g += (p >= plan.cols * t).astype(jnp.int32)
    j = p - plan.cols * g
    r = GROUP * g + i
    h = meta_ref[frame, 4] + r
    w = meta_ref[frame, 5] + j
    d = w - meta_ref[frame, 2]
    d = jnp.where(d < 0, d + plan.breadth, d)
    inside = (
        (r < plan.rows)
        & (p < plan.used)
        & (h >= meta_ref[frame, 0])
        & (h < meta_ref[frame, 0] + meta_ref[frame, 1])
        & (d < meta_ref[frame, 3])
    )
    return inside.astype(f32)


def load_tile(plan, ref, stage_ref, pack_ref, i):
    for g in range(plan.groups):
        r = GROUP * g + i
        at = slice(plan.padcol * g, plan.padcol * g + plan.cols)

        @pl.when(r < plan.rows)
        def _():
            stage_ref[at, :] = ref[0, r]

    return dot(pack_ref[...], stage_ref[...])


def store_tile(plan, ref, value, unpack_ref, i):
    spread = dot(unpack_ref[...], value).astype(bf16)
    for g in range(plan.groups):
        r = GROUP * g + i

        @pl.when(r < plan.rows)
        def _():
            ref[0, r] = spread[plan.padcol * g : plan.padcol * g + plan.cols]


def statistics(x):
    centre = jnp.mean(x, axis=-1, keepdims=True)
    centred = x - centre
    spread = jnp.mean(centred * centred, axis=-1, keepdims=True)
    r = lax.rsqrt(spread + epsilon)
    return centred * r, r


def norm_back(g, xhat, r):
    return r * (g - jnp.mean(g, axis=-1, keepdims=True) - xhat * jnp.mean(g * xhat, axis=-1, keepdims=True))


def join_blocks(plan, ref, i):
    at = slice(i * plan.size, (i + 1) * plan.size)
    return jnp.concatenate([ref[b, :, at] for b in range(plan.blocks)], axis=1)


def split_blocks(plan, ref, values):
    for b in range(plan.blocks):
        at = slice(b * plan.size, (b + 1) * plan.size)
        ref[b] = jnp.concatenate([v[:, at] for v in values], axis=1)


def first_kernel(plan, meta_ref, frames_ref, pack_ref, gain_ref, shift_ref, send_ref, stage_ref):
    frame = pl.program_id(0)
    stage_ref[...] = jnp.zeros_like(stage_ref)
    values = []
    for i in range(GROUP):
        if GROUP * (plan.groups - 1) + i >= plan.rows:
            stage_ref[plan.padcol * (plan.groups - 1) :, :] = jnp.zeros(
                (plan.padcol, plan.channels), bf16
            )
        inside = load_tile(plan, frames_ref, stage_ref, pack_ref, i) * token_mask(plan, meta_ref, frame, i)
        xhat, _ = statistics(inside)
        values.append((xhat * gain_ref[...] + shift_ref[...]).astype(bf16))
    split_blocks(plan, send_ref, values)


def first_call(plan, meta, frames, pack, gain, shift):
    tile = (1, plan.rows, plan.cols, plan.channels)
    return pl.pallas_call(
        functools.partial(first_kernel, plan),
        grid=(plan.micro,),
        in_specs=[
            pl.BlockSpec(memory_space=pltpu.SMEM),
            pl.BlockSpec(tile, lambda f: (f, 0, 0, 0)),
            full(pack.shape),
            full(gain.shape),
            full(shift.shape),
        ],
        out_specs=pl.BlockSpec((plan.blocks, plan.packed, plan.lanes), lambda f: (f, 0, 0)),
        out_shape=jax.ShapeDtypeStruct((plan.micro * plan.blocks, plan.packed, plan.lanes), bf16),
        scratch_shapes=[pltpu.VMEM((plan.stage, plan.channels), bf16)],
        compiler_params=params(48),
    )(meta, frames, pack, gain, shift)


def spectral_kernel(plan, middle, streams_in, streams_out, sums, *refs):
    (recv_ref, lon_ref, lon_back_ref, lat_ref, lat_back_ref, w_in_ref, w_out_ref, b_in_ref, b_out_ref), refs = (
        refs[:9],
        refs[9:],
    )
    ins, refs = refs[:streams_in], refs[streams_in:]
    send_ref, refs = refs[0], refs[1:]
    outs, refs = refs[:streams_out], refs[streams_out:]
    totals, refs = refs[:sums], refs[sums:]
    wide_ref, tall_ref = refs
    step = pl.program_id(0)
    groups, slots, breadth, win, size = plan.groups, plan.slots, plan.breadth, plan.window, plan.size
    kinds = 2 * breadth
    middle_steps = breadth // KSTEP

    def window_start(g):
        return pl.multiple_of(
            jnp.minimum(plan.cols * g // 16 * 16, plan.packed - win), 16
        )

    @pl.when(step == 0)
    def _():
        send_ref[...] = jnp.zeros_like(send_ref)
        for total in totals:
            total[...] = jnp.zeros_like(total)

    @pl.when(step < groups)
    def _():
        g = step
        ws = window_start(g)
        table = lon_ref[g]
        for lat in range(plan.lat):
            rows = jnp.concatenate(
                [recv_ref[lon * plan.lat + lat, pl.ds(ws, win), :] for lon in range(plan.lon)], axis=0
            )
            pad = jnp.zeros((plan.lon * win, LANES - size), bf16)
            for pair in range(GROUP // 2):
                pieces = []
                for i in (2 * pair, 2 * pair + 1):
                    pieces += [rows[:, i * size : (i + 1) * size], pad]
                out = dot(table, jnp.concatenate(pieces, axis=1)).astype(bf16).astype(f32)
                for n in range(2):
                    slot = lat * groups * GROUP + GROUP * g + 2 * pair + n
                    wide_ref[pl.ds(slot, kinds, stride=slots), :] = out[:, n * LANES : (n + 1) * LANES]

    @pl.when((step >= groups) & (step < groups + middle_steps))
    def _():
        first = (step - groups) * KSTEP
        spectra = []
        for pair in range(KSTEP // 2):
            columns = []
            for n in range(2):
                k = first + 2 * pair + n
                columns.append(
                    jnp.concatenate(
                        [
                            wide_ref[pl.ds(pl.multiple_of(k * slots, 8), slots), :],
                            wide_ref[pl.ds(pl.multiple_of((breadth + k) * slots, 8), slots), :],
                        ],
                        axis=0,
                    ).astype(bf16)
                )
            out = dot(lat_ref[...], jnp.concatenate(columns, axis=1)) * plan.scale
            for n in range(2):
                at = slice(n * LANES, (n + 1) * LANES)
                spectra.append(jnp.concatenate([out[:slots, at], out[slots:, at]], axis=1))
        result = middle(
            jnp.concatenate(spectra, axis=0), w_in_ref, w_out_ref, b_in_ref, b_out_ref, ins, outs, totals
        )
        for pair in range(KSTEP // 2):
            columns = []
            for n in range(2):
                at = slice((2 * pair + n) * slots, (2 * pair + n + 1) * slots)
                columns.append(jnp.concatenate([result[at, :LANES], result[at, LANES:]], axis=0))
            out = dot(lat_back_ref[...], jnp.concatenate(columns, axis=1)) * plan.scale
            out = out.astype(bf16).astype(f32)
            for n in range(2):
                k = first + 2 * pair + n
                at = slice(n * LANES, (n + 1) * LANES)
                tall_ref[pl.ds(k, slots, stride=kinds), :] = out[:slots, at]
                tall_ref[pl.ds(breadth + k, slots, stride=kinds), :] = out[slots:, at]

    @pl.when(step >= groups + middle_steps)
    def _():
        g = step - (groups + middle_steps)
        ws = window_start(g)
        table = lon_back_ref[g]
        for lat in range(plan.lat):
            pieces = []
            for pair in range(GROUP // 2):
                columns = []
                for i in (2 * pair, 2 * pair + 1):
                    slot = lat * groups * GROUP + GROUP * g + i
                    columns.append(tall_ref[pl.ds(pl.multiple_of(slot * kinds, 8), kinds), :].astype(bf16))
                out = dot(table, jnp.concatenate(columns, axis=1)).astype(bf16)
                pieces += [out[:, :size], out[:, LANES : LANES + size]]
            out = jnp.concatenate(pieces, axis=1)
            for lon in range(plan.lon):
                send_ref[lon * plan.lat + lat, pl.ds(ws, win), :] += out[lon * win : (lon + 1) * win]


def forward_middle(freq, w_in_ref, w_out_ref, b_in_ref, b_out_ref, ins, outs, totals):
    freq_ref, hid_ref, slope_ref = outs
    freq = freq.astype(bf16)
    freq_ref[...] = freq
    hid, slope = gelu_pair(dot(freq, w_in_ref[...]) + b_in_ref[...])
    hid = hid.astype(bf16)
    hid_ref[...] = hid
    slope_ref[...] = slope
    out = dot(hid, w_out_ref[...]) + b_out_ref[...]
    return (out - shrink_level * out * lax.rsqrt(out * out + shrink_level * shrink_level)).astype(bf16)


def backward_middle(grad_spec, w_in_ref, w_out_ref, b_in_ref, b_out_ref, ins, outs, totals):
    freq_ref, hid_ref, slope_ref = ins
    in_sum_ref, out_sum_ref, in_bias_ref, out_bias_ref = totals
    hid = hid_ref[...]
    out = dot(hid, w_out_ref[...]) + b_out_ref[...]
    r = lax.rsqrt(out * out + shrink_level * shrink_level)
    grad_out = (grad_spec * (1.0 - shrink_level**3 * (r * r * r))).astype(bf16)
    out_sum_ref[...] += dot_tn(hid, grad_out)
    out_bias_ref[...] += jnp.sum(grad_out.astype(f32), axis=0, keepdims=True)
    grad_pre = (dot_nt(grad_out, w_out_ref[...]) * slope_ref[...]).astype(bf16)
    in_sum_ref[...] += dot_tn(freq_ref[...], grad_pre)
    in_bias_ref[...] += jnp.sum(grad_pre.astype(f32), axis=0, keepdims=True)
    return dot_nt(grad_pre, w_in_ref[...]).astype(bf16)


def spectral_call(plan, middle, recv, tables, weights, streams_in, out_types, sums):
    middle_steps = plan.breadth // KSTEP
    rows = KSTEP * plan.slots
    consts = (recv,) + tables + weights
    stream = pl.BlockSpec((rows, 2 * LANES), lambda s: (jnp.clip(s - plan.groups, 0, middle_steps - 1), 0))
    sum_shapes = (
        [(2 * LANES, 2 * LANES)] * 2 + [(1, 2 * LANES)] * 2 if sums else []
    )
    total_rows = plan.breadth * plan.slots
    return pl.pallas_call(
        functools.partial(spectral_kernel, plan, middle, len(streams_in), len(out_types), len(sum_shapes)),
        grid=(plan.groups * 2 + middle_steps,),
        in_specs=[full(c.shape) for c in consts] + [stream] * len(streams_in),
        out_specs=[full(recv.shape)] + [stream] * len(out_types) + [full(s) for s in sum_shapes],
        out_shape=[jax.ShapeDtypeStruct(recv.shape, bf16)]
        + [jax.ShapeDtypeStruct((total_rows, 2 * LANES), t) for t in out_types]
        + [jax.ShapeDtypeStruct(s, f32) for s in sum_shapes],
        scratch_shapes=[
            pltpu.VMEM((2 * plan.breadth * plan.slots, LANES), f32),
            pltpu.VMEM((2 * plan.breadth * plan.slots, LANES), f32),
        ],
        compiler_params=params(60),
    )(*consts, *streams_in)


def block_matrix(plan, weight):
    pad = ((0, LANES - plan.size), (0, LANES - plan.size))
    real = jnp.pad(weight[0], pad)
    imag = jnp.pad(weight[1], pad)
    return jnp.concatenate(
        [jnp.concatenate([real, imag], axis=1), jnp.concatenate([-imag, real], axis=1)], axis=0
    )


def block_bias(plan, bias):
    return jnp.pad(bias.astype(f32), ((0, 0), (0, LANES - plan.size))).reshape(1, 2 * LANES)


FCHUNK = 512


def ffn_kernel(
    plan,
    hidden,
    meta_ref,
    frames_ref,
    cot_ref,
    recv_ref,
    pack_ref,
    unpack_ref,
    gain_one_ref,
    shift_one_ref,
    gain_two_ref,
    shift_two_ref,
    w_hidden_ref,
    b_hidden_ref,
    w_out_ref,
    b_out_ref,
    mixed_ref,
    send_ref,
    grad_mixed_ref,
    second_ref,
    branch_grad_ref,
    hid_ref,
    pre_grad_ref,
    gain_sum_ref,
    shift_sum_ref,
    out_bias_sum_ref,
    hidden_bias_sum_ref,
    stage_ref,
    filt_ref,
    keep_ref,
    branch_ref,
    grad_ref,
):
    frame, i = pl.program_id(0), pl.program_id(1)

    @pl.when((frame == 0) & (i == 0))
    def _():
        stage_ref[...] = jnp.zeros_like(stage_ref)
        for ref in (gain_sum_ref, shift_sum_ref, out_bias_sum_ref, hidden_bias_sum_ref):
            ref[...] = jnp.zeros_like(ref)

    @pl.when(i == 0)
    def _():
        for n in range(GROUP):
            filt_ref[n] = join_blocks(plan, recv_ref, n)

    mask = token_mask(plan, meta_ref, frame, i)
    inside = load_tile(plan, frames_ref, stage_ref, pack_ref, i) * mask
    xhat_one, _ = statistics(inside)
    normed = xhat_one * gain_one_ref[...] + shift_one_ref[...]
    mixed = filt_ref[i].astype(f32) + normed + inside
    xhat, r = statistics(mixed)
    second = (xhat * gain_two_ref[...] + shift_two_ref[...]).astype(bf16)
    second_ref[0] = second
    grad_out = load_tile(plan, cot_ref, stage_ref, pack_ref, i) * mask
    grad_branch = grad_out.astype(bf16)
    branch_grad_ref[0] = grad_branch
    out_bias_sum_ref[...] += jnp.sum(grad_branch.astype(f32), axis=0, keepdims=True)
    branch_ref[...] = jnp.zeros_like(branch_ref)
    grad_ref[...] = jnp.zeros_like(grad_ref)
    for c in range(hidden // FCHUNK):
        at = slice(c * FCHUNK, (c + 1) * FCHUNK)
        w_hidden = w_hidden_ref[at, :]
        w_out = w_out_ref[at, :]
        hid, slope = gelu_pair(dot_nt(second, w_hidden) + b_hidden_ref[:, at])
        hid = hid.astype(bf16)
        hid_ref[0, :, at] = hid
        branch_ref[...] += dot(hid, w_out)
        grad_pre = (dot_nt(grad_branch, w_out) * slope).astype(bf16)
        pre_grad_ref[0, :, at] = grad_pre
        hidden_bias_sum_ref[:, at] += jnp.sum(grad_pre.astype(f32), axis=0, keepdims=True)
        grad_ref[...] += dot(grad_pre, w_hidden)
    store_tile(
        plan, mixed_ref, ((mixed + branch_ref[...] + b_out_ref[...]) * mask).astype(bf16), unpack_ref, i
    )
    grad_second = grad_ref[...]
    gain_sum_ref[...] += jnp.sum(grad_second * xhat, axis=0, keepdims=True)
    shift_sum_ref[...] += jnp.sum(grad_second, axis=0, keepdims=True)
    grad_mixed = grad_out + norm_back(grad_second * gain_two_ref[...], xhat, r)
    grad_mixed_ref[0, 0] = grad_mixed
    keep_ref[i] = grad_mixed.astype(bf16)

    @pl.when(i == GROUP - 1)
    def _():
        split_blocks(plan, send_ref, [keep_ref[n] for n in range(GROUP)])


def ffn_call(plan, meta, frames, cot, recv, consts):
    hidden = consts[6].shape[0]
    tile = pl.BlockSpec((1, plan.rows, plan.cols, plan.channels), lambda f, i: (f, 0, 0, 0))
    packet = pl.BlockSpec((plan.blocks, plan.packed, plan.lanes), lambda f, i: (f, 0, 0))
    token = pl.BlockSpec((1, plan.packed, plan.channels), lambda f, i: (f * GROUP + i, 0, 0))
    wide = pl.BlockSpec((1, plan.packed, hidden), lambda f, i: (f * GROUP + i, 0, 0))
    tiles = plan.micro * GROUP
    sums = [(1, plan.channels)] * 3 + [(1, hidden)]
    return pl.pallas_call(
        functools.partial(ffn_kernel, plan, hidden),
        grid=(plan.micro, GROUP),
        in_specs=[pl.BlockSpec(memory_space=pltpu.SMEM), tile, tile, packet] + [full(c.shape) for c in consts],
        out_specs=[
            tile,
            packet,
            pl.BlockSpec((1, 1, plan.packed, plan.channels), lambda f, i: (f, i, 0, 0)),
            token,
            token,
            wide,
            wide,
        ]
        + [full(s) for s in sums],
        out_shape=[
            jax.ShapeDtypeStruct(frames.shape, bf16),
            jax.ShapeDtypeStruct(recv.shape, bf16),
            jax.ShapeDtypeStruct((plan.micro, GROUP, plan.packed, plan.channels), f32),
            jax.ShapeDtypeStruct((tiles, plan.packed, plan.channels), bf16),
            jax.ShapeDtypeStruct((tiles, plan.packed, plan.channels), bf16),
            jax.ShapeDtypeStruct((tiles, plan.packed, hidden), bf16),
            jax.ShapeDtypeStruct((tiles, plan.packed, hidden), bf16),
        ]
        + [jax.ShapeDtypeStruct(s, f32) for s in sums],
        scratch_shapes=[
            pltpu.VMEM((plan.stage, plan.channels), bf16),
            pltpu.VMEM((GROUP, plan.packed, plan.channels), bf16),
            pltpu.VMEM((GROUP, plan.packed, plan.channels), bf16),
            pltpu.VMEM((plan.packed, plan.channels), f32),
            pltpu.VMEM((plan.packed, plan.channels), f32),
        ],
        compiler_params=params(60),
    )(meta, frames, cot, recv, *consts)


def last_kernel(
    plan,
    meta_ref,
    frames_ref,
    recv_ref,
    grad_mixed_ref,
    pack_ref,
    unpack_ref,
    gain_ref,
    out_ref,
    gain_sum_ref,
    shift_sum_ref,
    stage_ref,
):
    frame = pl.program_id(0)

    @pl.when(frame == 0)
    def _():
        gain_sum_ref[...] = jnp.zeros_like(gain_sum_ref)
        shift_sum_ref[...] = jnp.zeros_like(shift_sum_ref)

    stage_ref[...] = jnp.zeros_like(stage_ref)
    for i in range(GROUP):
        mask = token_mask(plan, meta_ref, frame, i)
        inside = load_tile(plan, frames_ref, stage_ref, pack_ref, i) * mask
        xhat, r = statistics(inside)
        grad_mixed = grad_mixed_ref[0, i]
        grad_normed = join_blocks(plan, recv_ref, i).astype(f32) + grad_mixed
        gain_sum_ref[...] += jnp.sum(grad_normed * xhat, axis=0, keepdims=True)
        shift_sum_ref[...] += jnp.sum(grad_normed, axis=0, keepdims=True)
        grad_inside = grad_mixed + norm_back(grad_normed * gain_ref[...], xhat, r)
        store_tile(plan, out_ref, (grad_inside * mask).astype(bf16), unpack_ref, i)


def last_call(plan, meta, frames, recv, grad_mixed, consts):
    tile = pl.BlockSpec((1, plan.rows, plan.cols, plan.channels), lambda f: (f, 0, 0, 0))
    return pl.pallas_call(
        functools.partial(last_kernel, plan),
        grid=(plan.micro,),
        in_specs=[
            pl.BlockSpec(memory_space=pltpu.SMEM),
            tile,
            pl.BlockSpec((plan.blocks, plan.packed, plan.lanes), lambda f: (f, 0, 0)),
            pl.BlockSpec((1, GROUP, plan.packed, plan.channels), lambda f: (f, 0, 0, 0)),
        ]
        + [full(c.shape) for c in consts],
        out_specs=[tile, full((1, plan.channels)), full((1, plan.channels))],
        out_shape=[
            jax.ShapeDtypeStruct(frames.shape, bf16),
            jax.ShapeDtypeStruct((1, plan.channels), f32),
            jax.ShapeDtypeStruct((1, plan.channels), f32),
        ],
        scratch_shapes=[pltpu.VMEM((plan.stage, plan.channels), bf16)],
        compiler_params=params(56),
    )(meta, frames, recv, grad_mixed, *consts)


AXES = ("dp", "lon", "lat")


def exchange(values):
    return lax.all_to_all(values, ("lon", "lat"), 0, 0, tiled=True)


def reduce_over(values, axis):
    moved = lax.all_to_all(values.astype(bf16), axis, 0, 0, tiled=True)
    return jnp.sum(moved.astype(f32), axis=0)


def body(
    frames,
    regions,
    cotangent,
    first_gain,
    first_shift,
    inner_weight,
    inner_bias,
    outer_weight,
    outer_bias,
    second_gain,
    second_shift,
    hidden_weight,
    hidden_bias,
    output_weight,
    output_bias,
):
    dp, lon, lat = (lax.axis_size(a) for a in AXES)
    lon_place, lat_place = lax.axis_index("lon"), lax.axis_index("lat")
    micro, rows, cols, channels = frames.shape
    blocks = inner_weight.shape[0]
    plan = Plan(micro, rows, cols, channels, blocks, lat, lon)
    place = lon_place * lat + lat_place
    own_block = place % blocks
    hidden_rows = hidden_weight.shape[0]
    hidden = hidden_rows * dp * lon * lat

    origin = jnp.stack([lat_place * rows, lon_place * cols]).astype(jnp.int32)
    meta = jnp.concatenate([regions, jnp.broadcast_to(origin, (micro, 2))], axis=1)
    pack, unpack = (jnp.asarray(t) for t in pack_table(plan))
    tables = tuple(jnp.asarray(t) for t in lon_tables(plan) + lat_tables(plan))

    def row(v):
        return v.astype(f32).reshape(1, -1)

    def own(v):
        return lax.dynamic_index_in_dim(v, own_block, 0, keepdims=False)

    spectral_weights = (
        block_matrix(plan, own(inner_weight)),
        block_matrix(plan, own(outer_weight)),
        block_bias(plan, own(inner_bias)),
        block_bias(plan, own(outer_bias)),
    )

    bias_row = jnp.pad(hidden_bias.reshape(1, hidden_rows), ((0, 7), (0, channels - hidden_rows)))
    gathered = lax.all_gather(
        jnp.concatenate([hidden_weight, output_weight, bias_row], axis=0), AXES, axis=0
    )
    w_hidden = gathered[:, :hidden_rows].reshape(hidden, channels)
    w_output = gathered[:, hidden_rows : 2 * hidden_rows].reshape(hidden, channels)
    b_hidden = gathered[:, 2 * hidden_rows, :hidden_rows].astype(f32).reshape(1, hidden)

    send = first_call(plan, meta, frames, pack, row(first_gain), row(first_shift))
    send, freq, hid, slope = spectral_call(
        plan, forward_middle, exchange(send), tables, spectral_weights, (), (bf16, bf16, f32), False
    )
    (
        mixed_frames,
        send,
        grad_mixed,
        second,
        grad_branch,
        hidden_act,
        grad_preact,
        second_gain_sum,
        second_shift_sum,
        output_bias_sum,
        hidden_bias_sum,
    ) = ffn_call(
        plan,
        meta,
        frames,
        cotangent,
        exchange(send),
        (
            pack,
            unpack,
            row(first_gain),
            row(first_shift),
            row(second_gain),
            row(second_shift),
            w_hidden,
            b_hidden,
            w_output,
            row(output_bias),
        ),
    )
    received = exchange(send)

    def weight_grad(left, right):
        return jnp.einsum("atf,atc->fc", left, right, preferred_element_type=f32)

    weight_sums = jnp.stack(
        [
            weight_grad(grad_preact, second).reshape(dp, lon, lat, hidden_rows, channels),
            weight_grad(hidden_act, grad_branch).reshape(dp, lon, lat, hidden_rows, channels),
        ],
        axis=3,
    )
    ffn_grads = reduce_over(reduce_over(reduce_over(weight_sums, "dp"), "lon"), "lat")

    send, inner_sum, outer_sum, inner_bias_sum, outer_bias_sum = spectral_call(
        plan, backward_middle, received, tables, spectral_weights, (freq, hid, slope), (), True
    )
    frame_grad, first_gain_sum, first_shift_sum = last_call(
        plan, meta, frames, exchange(send), grad_mixed, (pack, unpack, row(first_gain))
    )

    def spread(value):
        return lax.dynamic_update_slice_in_dim(
            jnp.zeros((blocks,) + value.shape, f32), value[None], own_block, 0
        )

    def complex_sum(full_sum):
        s = plan.size
        rr, ri = full_sum[:s, :s], full_sum[:s, LANES : LANES + s]
        ir, ii = full_sum[LANES : LANES + s, :s], full_sum[LANES : LANES + s, LANES : LANES + s]
        return spread(jnp.stack([rr + ii, ri - ir]))

    def bias_sum(full_sum):
        return spread(full_sum.reshape(2, LANES)[:, : plan.size])

    sums = lax.psum(
        (
            first_gain_sum,
            first_shift_sum,
            complex_sum(inner_sum),
            bias_sum(inner_bias_sum),
            complex_sum(outer_sum),
            bias_sum(outer_bias_sum),
            second_gain_sum,
            second_shift_sum,
            hidden_bias_sum,
            output_bias_sum,
        ),
        AXES,
    )
    order = lax.axis_index(AXES)
    hidden_bias_grad = lax.dynamic_slice_in_dim(sums[8].reshape(hidden), order * hidden_rows, hidden_rows, 0)
    flat = lambda v: v.reshape(channels)
    return (
        mixed_frames,
        frame_grad,
        flat(sums[0]),
        flat(sums[1]),
        sums[2],
        sums[3],
        sums[4],
        sums[5],
        flat(sums[6]),
        flat(sums[7]),
        ffn_grads[0],
        hidden_bias_grad,
        ffn_grads[1],
        flat(sums[9]),
    )


def solution(mesh):
    field = P("dp", "lat", "lon", None)
    rows = P(AXES, None)
    return jax.shard_map(
        body,
        mesh=mesh,
        in_specs=(field, P("dp", None), field) + (P(),) * 8 + (rows, P(AXES), rows, P()),
        out_specs=(field, field) + (P(),) * 8 + (rows, P(AXES), rows, P()),
        check_vma=False,
    )
```

time: 2800 us -> 859 us (0.31)
  waiting for transfers between devices: 1140 us -> 340 us
  local copies, waits for them, and re-layouts: 549 us -> 49.8 us
  matrix products: 511 us -> 30.1 us
  blocking collectives: 444 us -> 116 us
  Pallas kernels: 0 us -> 243 us
  other arithmetic: 73.8 us -> 32.1 us
    all_gather x16 -> x1, waiting for transfers between devices: 551 us -> 0.01 us  [body(): lax.all_gather(jnp.concatenate([hidden_weight, output_weight, bias_row],...]
    dot_general x108 -> x2, matrix products: 511 us -> 30.1 us  [weight_grad(): return jnp.einsum('atf,atc->fc', left, right, preferred_element_type=f32)]
    reduce_scatter x2 -> x0, waiting for transfers between devices: 283 us -> none  [the longest x1 142 us: body(): lax.psum_scatter(totals[2], ('dp', 'lon', 'lat'), scatter_dimension=0, ti...]
    all_to_all x6 -> x2, blocking collectives: 326 us -> 77.8 us  [reduce_over(): moved = lax.all_to_all(values.astype(bf16), axis, 0, 0, tiled=True)]
    pallas_call x0 -> x5, Pallas kernels: none -> 243 us  [the longest x2 140 us: spectral_call(): pl.pallas_call(functools.partial(spectral_kernel, plan, middle, len(strea...]
    all_to_all x40 -> x0, local copies, waits for them, and re-layouts: 180 us -> none  [the longest x6 34.5 us: step(): lax.all_to_all(lon_imag.astype(jnp.bfloat16), 'lat', split_axis=2, concat...]
    while x420 -> x0, local copies, waits for them, and re-layouts: 169 us -> none
    convert_element_type x30 -> x2, local copies, waits for them, and re-layouts: 125 us -> 1.37 us  [the longest x1 0.68 us: body(): gathered[:, 2 * hidden_rows, :hidden_rows].astype(f32).reshape(1, hidden)]
  transfers between devices with their start and end apart: 29 -> 7, of which waited for: 25 -> 5; matrix products, arithmetic and copies ran while one was open for 16% -> 6% of each run, Pallas kernels for 0% -> 19%
where the time goes in v1:
time: 859 us; the launch traced here: 852 us
  waiting for transfers between devices  340 us (40%)
  Pallas kernels  243 us (28%)
  blocking collectives  116 us (14%)
  local copies, waits for them, and re-layouts  49.8 us (6%)
  other arithmetic  32.1 us (4%)
  matrix products  30.1 us (4%)
  starting transfers between devices  26.4 us (3%)
  between operations  14.9 us (2%)
    all_to_all x4, waiting for transfers between devices, exchange(): return lax.all_to_all(values, ('lon', 'lat'), 0, 0, tiled=True)  312 us
    pallas_call x2, Pallas kernels, spectral_call(): pl.pallas_call(functools.partial(spectral_kernel, plan, middle, len(strea...  140 us
    pallas_call x1, Pallas kernels, ffn_call(): pl.pallas_call(functools.partial(ffn_kernel, plan, hidden), grid=(plan.mi...  80.2 us
    all_to_all x2, blocking collectives, reduce_over(): moved = lax.all_to_all(values.astype(bf16), axis, 0, 0, tiled=True)  77.8 us
    psum x1, blocking collectives, body(): lax.psum((first_gain_sum, first_shift_sum, complex_sum(inner_sum), bias_s...  38.4 us
    dot_general x2, matrix products, weight_grad(): return jnp.einsum('atf,atc->fc', left, right, preferred_element_type=f32)  30.1 us
    unnamed x52, local copies, waits for them, and re-layouts  28.3 us
    psum x1, waiting for transfers between devices, body(): lax.psum((first_gain_sum, first_shift_sum, complex_sum(inner_sum), bias_s...  27.2 us
  transfers between devices with their start and end apart: 7, of which 5 were waited for; matrix products, arithmetic and copies ran while one was open for 6% of the time, Pallas kernels for 19%

profile of v1, /device:TPU:0, one launch (start us, length us, event | category | flops | bytes accessed | tf_op | source)
XLA Modules:
  0.0 851.7 jit_solution(12828312503106098710)
XLA Ops:
  13.6 7.9 shard_map.308
  21.5 8.4 all-to-all-start
  33.8 113.1 %all-to-all-done.refs_0_ = bf16[16,272,384]{2,1,0:T(8,128)(2,1)} async-done(((bf16[16,272,384]{2,1,0:T(8,128)(2,1)}), bf16[16,272,384]{2,1,0:T(8,128)(2,1)}, u32[]{:S(2)}, u32[]{:S(2)}) %all-to-all-start) | async-done | bytes 3342368 | tf_op jit(solution)/shard_map/all_to_all | solution.py:577
  146.9 67.0 %shard_map.309 = (bf16[16,272,384]{2,1,0:T(8,128)(2,1)}, bf16[17280,256]{1,0:T(8,128)(2,1)}, bf16[17280,256]{1,0:T(8,128)(2,1)}, f32[17280,256]{1,0:T(8,128)}) custom-call(bf16[16,272,384]{2,1,0:T(8,128)(2,1)} %all-to-all-done.refs_0_, bf16[6,360,256]{2,1,0:T(8,128)(2,1)} %constant.76.clone.refs_1_, bf16[6,256,360]{2,1,0:T(8,128)(2,1)} %constant.77.clone.refs_2_, ...), custom_call_target="tpu_custom_call" | custom-call | tf_op jit(solution)/shard_map/pallas_call | solution.py:353
  225.6 8.0 fusion.8
  233.6 60.5 %all-to-all-done.1.recv_ref = bf16[16,272,384]{2,1,0:T(8,128)(2,1)S(1)} async-done(((bf16[16,272,384]{2,1,0:T(8,128)(2,1)}), bf16[16,272,384]{2,1,0:T(8,128)(2,1)S(1)}, u32[]{:S(2)}, u32[]{:S(2)}) %all-to-all-start.1) | async-done | bytes 3342368 | tf_op jit(solution)/shard_map/all_to_all | solution.py:577
  295.9 80.2 %shard_map.310 = (bf16[2,23,45,768]{3,2,1,0:T(8,128)(2,1)}, bf16[16,272,384]{2,1,0:T(8,128)(2,1)}, f32[2,4,272,768]{3,2,1,0:T(8,128)}, bf16[8,272,768]{2,1,0:T(8...) custom-call(s32[2,6]{1,0:T(2,128)} %copy-done.3, ...), custom_call_target="tpu_custom_call" | custom-call | tf_op jit(solution)/shard_map/pallas_call | solution.py:481
  376.1 17.1 %bitcast_convert_fusion.1 = bf16[3072,768]{1,0:T(8,128)(2,1)} fusion(bf16[8,272,3072]{2,1,0:T(8,128)(2,1)} %get-tuple-element.54, bf16[8,272,768]{2,1,0:T(8,128)(2,1)} %get-tuple-element.55), kind=kOutput, calls=%fused_computation.2 | convolution fusion | flops 10270015488 | bytes 21430272 | tf_op jit(solution)/shard_map/atf,atc->fc/dot_general | solution.py:676
  393.2 12.9 %bitcast_convert_fusion = bf16[3072,768]{1,0:T(8,128)(2,1)} fusion(bf16[8,272,3072]{2,1,0:T(8,128)(2,1)S(1)} %copy-done.21, bf16[8,272,768]{2,1,0:T(8,128)(2,1)S(1)} %copy-done.22), kind=kOutput, calls=%fused_computation.1 | convolution fusion | flops 10270015488 | bytes 21430272 | tf_op jit(solution)/shard_map/atf,atc->fc/dot_general | solution.py:676
  406.2 8.3 pad_maximum_fusion
  414.5 20.3 %all_to_all.35 = bf16[2,4,4,2,96,768]{5,4,2,1,3,0:T(8,128)(2,1)} all-to-all(bf16[2,4,4,2,96,768]{5,4,2,1,3,0:T(8,128)(2,1)} %pad_maximum_fusion), channel_id=1, replica_groups=mesh['dp'=2,'lon'=4,'lat'=4] {'dp'}, dimensions={0} | all-to-all | bytes 18874368 | tf_op jit(solution)/shard_map/all_to_all | solution.py:581
  434.8 9.1 %reduce_sum.33 = bf16[4,4,2,96,768]{4,3,1,0,2:T(8,128)(2,1)} reduce(bf16[2,4,4,2,96,768]{5,4,2,1,3,0:T(8,128)(2,1)} %all_to_all.35, bf16[]{:T(256)} %constant.67.clone.1), dimensions={0}, to_apply=%region_8.9 | reduce | flops 2359296 | bytes 14155778 | tf_op jit(solution)/shard_map/reduce_sum | solution.py:582
  446.6 57.5 %all_to_all.36 = bf16[4,4,2,96,768]{4,3,1,2,0:T(8,128)(2,1)} all-to-all(bf16[4,4,2,96,768]{4,3,1,2,0:T(8,128)(2,1)S(1)} %copy.68), channel_id=1, replica_groups=mesh['dp'=2,'lon'=4,'lat'=4] {'lon'}, dimensions={0} | all-to-all | bytes 9437184 | tf_op jit(solution)/shard_map/all_to_all | solution.py:581
  507.8 4.4 reduce_sum.34
  514.6 69.2 %all-to-all-done.2.refs_0_ = bf16[16,272,384]{2,1,0:T(8,128)(2,1)S(1)} async-done(((bf16[16,272,384]{2,1,0:T(8,128)(2,1)}), bf16[16,272,384]{2,1,0:T(8,128)(2,1)S(1)}, u32[]{:S(2)}, u32[]{:S(2)}) %all-to-all-start.2) | async-done | bytes 3342368 | tf_op jit(solution)/shard_map/all_to_all | solution.py:577
  583.8 4.3 all-to-all-start.6
  588.1 73.3 %shard_map.311 = (bf16[16,272,384]{2,1,0:T(8,128)(2,1)}, f32[256,256]{1,0:T(8,128)}, f32[256,256]{1,0:T(8,128)}, f32[1,256]{1,0:T(1,128)}, f32[1,256]{1,0:T(1,128)}) custom-call(bf16[16,272,384]{2,1,0:T(8,128)(2,1)} %copy-done.5, bf16[6,360,256]{2,1,0:T(8,128)(2,1)} %constant.76.clone.refs_1_, bf16[6,256,360]{2,1,0:T(8,128)(2,1)} %constant.77.clone.refs_2_, ...), custom_call_target="tpu_custom_call" | custom-call | tf_op jit(solution)/shard_map/pallas_call | solution.py:353
  661.5 5.4 all-to-all-start.3
  667.4 6.2 copy.71
  681.1 69.6 %all-to-all-done.3.recv_ref = bf16[16,272,384]{2,1,0:T(8,128)(2,1)S(1)} async-done(((bf16[16,272,384]{2,1,0:T(8,128)(2,1)}), bf16[16,272,384]{2,1,0:T(8,128)(2,1)S(1)}, u32[]{:S(2)}, u32[]{:S(2)}) %all-to-all-start.3) | async-done | bytes 3342368 | tf_op jit(solution)/shard_map/all_to_all | solution.py:577
  752.4 14.2 %shard_map.312 = (bf16[2,23,45,768]{3,2,1,0:T(8,128)(2,1)}, f32[1,768]{1,0:T(1,128)}, f32[1,768]{1,0:T(1,128)}) custom-call(s32[2,6]{1,0:T(2,128)} %copy-done.3, bf16[2,23,45,768]{3,2,1,0:T(8,128)(2,1)} %copy.62.frames_ref, bf16[16,272,384]{2,1,0:T(8,128)(2,1)} %copy-done.6, f32[2,4,272,768]{3,2,1,0:T(8,128)} %get-tuple-element.44.grad_mixed_ref, ...), custom_call_target="tpu_custom_call" | custom-call | tf_op jit(solution)/shard_map/pallas_call | solution.py:552
  768.1 6.1 copy.72
  774.2 38.4 %all-reduce.7 = (f32[768]{0:T(1024)}, f32[768]{0:T(1024)}, f32[8,2,96]{2,1,0:T(2,128)}, f32[8,2,96]{2,1,0:T(2,128)}, f32[768]{0:T(1024)}, /*index=5*/f32[768]{0:T(1024)}, f32[1,3072]{1,0:T(1,128)S(1)}, f32[768]{0:T(1024)}) all-reduce(f32[768]{0:T(1024)S(1)} %reduce.3, ...), channel_id=1, replica_groups=mesh['dp'=2,'lon'=4,'lat'=4] {'dp','lon','lat'}, use_global_device_ids=true, to_apply=%region_0.1 | all-reduce | flops 9984 | bytes 79872 | tf_op jit(solution)/shard_map/psum | solution.py:708
  813.1 27.2 %all-reduce.11.cloned.1.call-done = (f32[8,2,96,96]{3,2,1,0:T(8,128)}, f32[8,2,96,96]{3,2,1,0:T(8,128)}) async-done(((f32[8,2,96,96]{3,2,1,0:T(8,128)}, f32[8,2,96,96]{3,2,1,0:T(8,128)}), (f32[8,2,96,96]{3,2,1,0:T(8,128)}, f32[8,2,96,96]{3,2,1,0:T(8,128)})) %all-reduce.11.cloned.1.call-update) | async-done | bytes 1179664 | tf_op jit(solution)/shard_map/psum | solution.py:708
  (99 shorter events, 48.1 us)
Async XLA Ops:
  7.2 6.4 copy-start
  7.2 6.1 copy-start.13
  7.2 6.1 copy-start.14
  7.2 6.3 copy-start.18
  7.2 216.8 %all-gather.3.cloned.1.call-start = ((), (), s32[]{:S(2)}) async-start(), calls=%async_computation.7 | async-start | bytes 10137600 | tf_op jit(solution)/shard_map/all_gather | solution.py:631
  13.3 8.1 copy-start.1
  13.4 8.1 copy-start.2
  13.6 7.9 copy-start.3
  21.5 125.4 %all-to-all-start = ((bf16[16,272,384]{2,1,0:T(8,128)(2,1)}), bf16[16,272,384]{2,1,0:T(8,128)(2,1)}, u32[]{:S(2)}, u32[]{:S(2)}) async-start(bf16[16,272,384]{2,1,0:T(8,128)(2,1)} %shard_map.308), calls=%async_computation | async-start | bytes 6684672 | tf_op jit(solution)/shard_map/all_to_all | solution.py:577
  213.9 80.2 %all-to-all-start.1 = ((bf16[16,272,384]{2,1,0:T(8,128)(2,1)}), bf16[16,272,384]{2,1,0:T(8,128)(2,1)S(1)}, u32[]{:S(2)}, u32[]{:S(2)}) async-start(bf16[16,272,384]{2,1,0:T(8,128)(2,1)} %get-tuple-element.37), calls=%async_computation.1 | async-start | bytes 6684672 | tf_op jit(solution)/shard_map/all_to_all | solution.py:577
  376.1 17.2 %copy-start.21 = (bf16[8,272,3072]{2,1,0:T(8,128)(2,1)S(1)}, bf16[8,272,3072]{2,1,0:T(8,128)(2,1)}, u32[]{:S(2)}) copy-start(bf16[8,272,3072]{2,1,0:T(8,128)(2,1)} %get-tuple-element.56) | copy-start | bytes 40108036
  376.1 17.2 %copy-start.22 = (bf16[8,272,768]{2,1,0:T(8,128)(2,1)S(1)}, bf16[8,272,768]{2,1,0:T(8,128)(2,1)}, u32[]{:S(2)}) copy-start(bf16[8,272,768]{2,1,0:T(8,128)(2,1)} %get-tuple-element.57) | copy-start | bytes 10027012
  504.1 79.7 %all-to-all-start.2 = ((bf16[16,272,384]{2,1,0:T(8,128)(2,1)}), bf16[16,272,384]{2,1,0:T(8,128)(2,1)S(1)}, u32[]{:S(2)}, u32[]{:S(2)}) async-start(bf16[16,272,384]{2,1,0:T(8,128)(2,1)} %get-tuple-element.39), calls=%async_computation.2 | async-start | bytes 6684672 | tf_op jit(solution)/shard_map/all_to_all | solution.py:577
  583.8 77.7 %all-to-all-start.6 = ((bf16[4,2,96,768]{3,2,1,0:T(8,128)(2,1)}), bf16[4,2,96,768]{3,2,1,0:T(8,128)(2,1)}, u32[]{:S(2)}, u32[]{:S(2)}) async-start(bf16[4,2,96,768]{3,2,1,0:T(8,128)(2,1)} %copy.70), calls=%async_computation.6 | async-start | bytes 2359296 | tf_op jit(solution)/shard_map/all_to_all | solution.py:581
  661.5 5.8 copy-start.12
  661.5 5.8 copy-start.11
  661.5 5.8 copy-start.10
  661.5 89.2 %all-to-all-start.3 = ((bf16[16,272,384]{2,1,0:T(8,128)(2,1)}), bf16[16,272,384]{2,1,0:T(8,128)(2,1)S(1)}, u32[]{:S(2)}, u32[]{:S(2)}) async-start(bf16[16,272,384]{2,1,0:T(8,128)(2,1)} %get-tuple-element.43), calls=%async_computation.3 | async-start | bytes 6684672 | tf_op jit(solution)/shard_map/all_to_all | solution.py:577
  666.9 173.4 %all-reduce.11.cloned.1.call-start = ((), (), s32[]{:S(2)}) async-start(), calls=%async_computation.8 | async-start | bytes 3145728 | tf_op jit(solution)/shard_map/psum | solution.py:708
  667.3 8.5 copy-start.8
  667.3 10.1 %copy-start.7 = (f32[256,256]{1,0:T(8,128)S(1)}, f32[256,256]{1,0:T(8,128)}, u32[]{:S(2)}) copy-start(f32[256,256]{1,0:T(8,128)} %get-tuple-element.48) | copy-start | bytes 786436
  673.5 7.5 copy-start.20
  673.5 7.5 copy-start.19
  766.6 7.5 copy-start.9
  (6 other events, 22.0 us)
Sparse Core Ops, SparseCore 0:
  11.4 138.9 all-gather.2
  679.2 160.9 all-reduce.10

commit v2 on v1

v2 whole, which is shorter than its diff:
```python
import functools
import math

import jax
import jax.numpy as jnp
import numpy as np
from jax import lax
from jax.experimental import pallas as pl
from jax.experimental.pallas import tpu as pltpu
from jax.sharding import PartitionSpec as P

H = 90
LANES = 128
GROUP = 4
HALVES = 2
MAX_KSTEP = 12
HINT = 0.05

epsilon = 1e-05
shrink_level = 0.01

f32 = jnp.float32
bf16 = jnp.bfloat16


class Plan:
    def __init__(self, micro, rows, cols, channels, blocks, lat, lon):
        self.micro, self.rows, self.cols, self.channels, self.blocks = micro, rows, cols, channels, blocks
        self.lat, self.lon = lat, lon
        self.places = lat * lon
        self.size = channels // blocks
        self.groups = -(-rows // (GROUP * HALVES))
        self.padcol = -(-cols // 16) * 16
        self.packed = self.groups * self.padcol
        self.part = self.groups * GROUP
        self.slots = lat * self.part
        self.pitch = odd_pitch(self.slots)
        self.height = rows * lat
        self.breadth = cols * lon
        self.waves = self.breadth // HALVES
        self.padwave = -(-self.waves // 16) * 16
        self.lanes = GROUP * self.size
        self.scale = float(H * self.breadth) ** (-0.5)
        self.kstep = max(k for k in range(2, MAX_KSTEP + 1, 2) if self.waves % k == 0)


def odd_pitch(rows):
    rows = -(-rows // 8) * 8
    return rows + 8 if rows % 16 == 0 else rows


def angle_tables(count, total):
    index = np.arange(total)
    turns = (index[:, None] * index[None, :]) % count
    angle = turns * (2.0 * math.pi / count)
    keep = ((index[:, None] < count) & (index[None, :] < count)).astype(np.float64)
    return np.cos(angle) * keep, np.sin(angle) * keep


def lon_tables(plan):
    cos, sin = angle_tables(plan.breadth, plan.breadth)
    width = plan.lon * plan.padcol
    out = np.zeros((2, plan.breadth, width), np.float32)
    for s in range(plan.lon):
        w = slice(s * plan.cols, (s + 1) * plan.cols)
        at = slice(s * plan.padcol, s * plan.padcol + plan.cols)
        out[0, :, at] = cos[:, w]
        out[1, :, at] = -sin[:, w]
    back = np.zeros((2, width, 2, 2, plan.padwave), np.float32)
    for d in range(2):
        for n in range(2):
            half = (d + n) % 2
            waves = slice(half * plan.waves, (half + 1) * plan.waves)
            for kind in range(2):
                back[d, :, n, kind, : plan.waves] = out[kind, waves].T
    return out.reshape(2 * plan.breadth, width).astype(jnp.bfloat16), back.reshape(2, width, -1).astype(jnp.bfloat16)


def lat_tables(plan):
    cos, sin = angle_tables(H, plan.height)
    n = HALVES * plan.slots
    forward, inverse = [], []
    for d in range(2):
        c = np.zeros((n, n))
        s = np.zeros((n, n))
        for order in range(2):
            half = (d + order) % 2
            for lat in range(plan.lat):
                for r in range(plan.part):
                    row = half * plan.part + r
                    if row < plan.rows:
                        at = order * plan.slots + lat * plan.part + r
                        c[: plan.height, at] = cos[:, lat * plan.rows + row]
                        s[: plan.height, at] = sin[:, lat * plan.rows + row]
        forward.append(np.block([[c, s], [-s, c]]))
        inverse.append(np.block([[c.T, -s.T], [s.T, c.T]]))
    return tuple(np.stack(t).astype(np.float32).astype(jnp.bfloat16) for t in (forward, inverse))


def dot(a, b):
    return lax.dot_general(a, b, (((1,), (0,)), ((), ())), preferred_element_type=f32)


def dot_nt(a, b):
    return lax.dot_general(a, b, (((1,), (1,)), ((), ())), preferred_element_type=f32)


def dot_tn(a, b):
    return lax.dot_general(a, b, (((0,), (0,)), ((), ())), preferred_element_type=f32)


def gelu_pair(x):
    phi = 0.5 + 0.5 * lax.erf(x * (0.5**0.5))
    density = jnp.exp(-0.5 * x * x) * (1.0 / math.sqrt(2.0 * math.pi))
    return x * phi, phi + x * density


def full(shape):
    return pl.BlockSpec(shape, lambda *_: (0,) * len(shape), pipeline_mode=pl.Buffered(1))


def params(mib):
    return pltpu.CompilerParams(vmem_limit_bytes=mib * 2**20)


def cost(flops, moved):
    return pl.CostEstimate(flops=int(flops * HINT), bytes_accessed=int(moved * HINT), transcendentals=0)


def bump(ref, value):
    ref[...] += jnp.sum(value, axis=0, keepdims=True)


def row_mask(plan, meta_ref, half, i):
    p = lax.broadcasted_iota(jnp.int32, (plan.packed, 1), 0)
    g = jnp.zeros_like(p)
    for t in range(1, plan.groups):
        g += (p >= plan.padcol * t).astype(jnp.int32)
    j = p - plan.padcol * g
    r = plan.part * half + GROUP * g + i
    h = meta_ref[4] + r
    w = meta_ref[5] + j
    d = w - meta_ref[2]
    d = jnp.where(d < 0, d + plan.breadth, d)
    inside = (
        (r < plan.rows)
        & (j < plan.cols)
        & (h >= meta_ref[0])
        & (h < meta_ref[0] + meta_ref[1])
        & (d < meta_ref[3])
    )
    return inside.astype(f32)


def load_row(plan, ref, half, i):
    base = plan.part * half + i
    return jnp.concatenate([ref[0, base + GROUP * g] for g in range(plan.groups)], axis=0)


def store_row(plan, ref, value, half, i):
    base = plan.part * half + i
    for g in range(plan.groups):
        ref[base + GROUP * g] = value[plan.padcol * g : plan.padcol * (g + 1)]


def statistics(x):
    centre = jnp.mean(x, axis=-1, keepdims=True)
    centred = x - centre
    spread = jnp.mean(centred * centred, axis=-1, keepdims=True)
    r = lax.rsqrt(spread + epsilon)
    return centred * r, r


def norm_back(g, xhat, r):
    return r * (g - jnp.mean(g, axis=-1, keepdims=True) - xhat * jnp.mean(g * xhat, axis=-1, keepdims=True))


def join_blocks(plan, ref, first, i):
    at = slice(i * plan.size, (i + 1) * plan.size)
    return jnp.concatenate([ref[first + b, :, at] for b in range(plan.blocks)], axis=1)


def split_blocks(plan, ref, first, values):
    for b in range(plan.blocks):
        at = slice(b * plan.size, (b + 1) * plan.size)
        ref[first + b] = jnp.concatenate([v[:, at] for v in values], axis=1)


SCALARS = pl.BlockSpec(memory_space=pltpu.SMEM)


def tile_spec(plan, slot):
    return pl.BlockSpec(
        (1, HALVES * plan.part, plan.padcol, plan.channels),
        lambda *_: (slot, 0, 0, 0),
        pipeline_mode=pl.Buffered(1),
    )


def tile_shape(plan):
    return jax.ShapeDtypeStruct((HALVES * plan.part, plan.padcol, plan.channels), bf16)


def packet_shape(plan, count):
    return jax.ShapeDtypeStruct((count, plan.packed, plan.lanes), bf16)


def first_kernel(plan, meta_ref, frames_ref, gain_ref, shift_ref, send_ref, give_ref):
    d = meta_ref[6]
    for n, ref, first in ((0, send_ref, d * plan.blocks), (1, give_ref, 0)):
        half = d if n == 0 else 1 - d
        values = []
        for i in range(GROUP):
            inside = load_row(plan, frames_ref, half, i).astype(f32) * row_mask(plan, meta_ref, half, i)
            xhat, _ = statistics(inside)
            values.append((xhat * gain_ref[...] + shift_ref[...]).astype(bf16))
        split_blocks(plan, ref, first, values)


def first_call(plan, slot, meta, frames, gain, shift):
    shapes = [packet_shape(plan, plan.places), packet_shape(plan, plan.blocks)]
    return pl.pallas_call(
        functools.partial(first_kernel, plan),
        grid=(1,),
        in_specs=[SCALARS, tile_spec(plan, slot), full(gain.shape), full(shift.shape)],
        out_specs=[full(v.shape) for v in shapes],
        out_shape=shapes,
        compiler_params=params(32),
        cost_estimate=cost(5e9, 8e6),
    )(meta, frames, gain, shift)


def lon_kernel(plan, meta_ref, recv_ref, table_ref, keep_ref, give_ref, wide_ref):
    g = pl.program_id(0)
    kinds, size, pad = 2 * plan.breadth, plan.size, plan.padcol
    at = pl.ds(pl.multiple_of(g * pad, 16), pad)
    gap = jnp.zeros((plan.lon * pad, LANES - size), bf16)
    for lat in range(plan.lat):
        rows = jnp.concatenate([recv_ref[lon * plan.lat + lat, at, :] for lon in range(plan.lon)], axis=0)
        for pair in range(GROUP // 2):
            pieces = []
            for i in (2 * pair, 2 * pair + 1):
                pieces += [rows[:, i * size : (i + 1) * size], gap]
            out = dot(table_ref[...], jnp.concatenate(pieces, axis=1))
            for n in range(2):
                slot = lat * plan.part + GROUP * g + 2 * pair + n
                wide_ref[pl.ds(slot, kinds, stride=plan.pitch), :] = out[:, n * LANES : (n + 1) * LANES]

    @pl.when(g == plan.groups - 1)
    def _():
        d = meta_ref[6]
        for ref, half in ((keep_ref, d), (give_ref, 1 - d)):
            for kind in range(2):
                base = kind * plan.breadth + half * plan.waves

                def move(k, _, ref=ref, kind=kind, base=base):
                    row = pl.multiple_of((base + k) * plan.pitch, 8)
                    to = pl.multiple_of(k * plan.slots, 16)
                    ref[kind, pl.ds(to, plan.slots), :] = wide_ref[pl.ds(row, plan.slots), :].astype(bf16)
                    return _

                lax.fori_loop(0, plan.waves, move, 0, unroll=10)


def lon_call(plan, meta, recv, table):
    shape = jax.ShapeDtypeStruct((2, plan.waves * plan.slots, LANES), bf16)
    return pl.pallas_call(
        functools.partial(lon_kernel, plan),
        grid=(plan.groups,),
        in_specs=[SCALARS, full(recv.shape), full(table.shape)],
        out_specs=[full(shape.shape)] * 2,
        out_shape=[shape] * 2,
        scratch_shapes=[pltpu.VMEM((2 * plan.breadth * plan.pitch, LANES), f32)],
        compiler_params=params(40),
        cost_estimate=cost(4e9, 8e6),
    )(meta, recv, table)


def wave_kernel(plan, middle, counts, *refs):
    refs = list(refs)

    def take(n):
        got = tuple(refs[:n])
        del refs[:n]
        return got

    mine_ref, other_ref, lat_ref, lat_back_ref = take(4)
    weights = take(4)
    ins = take(counts[0])
    back_refs = take(2)
    outs = take(counts[1])
    totals = take(counts[2])
    tall_refs = refs[:2]
    sums_ref = totals[0] if totals else None
    totals = tuple(refs[2:])
    step = pl.program_id(0)
    slots, pitch = plan.slots, odd_pitch(2 * plan.padwave)
    both = HALVES * slots

    @pl.when(step == 0)
    def _():
        for ref in totals + tuple(tall_refs):
            ref[...] = jnp.zeros_like(ref)

    spectra = []
    for pair in range(plan.kstep // 2):
        columns = []
        for n in range(2):
            at = slice((2 * pair + n) * slots, (2 * pair + n + 1) * slots)
            columns.append(
                jnp.concatenate([ref[kind, at, :] for kind in range(2) for ref in (mine_ref, other_ref)], axis=0)
            )
        out = dot(lat_ref[...], jnp.concatenate(columns, axis=1)) * plan.scale
        for n in range(2):
            at = slice(n * LANES, (n + 1) * LANES)
            spectra.append(jnp.concatenate([out[:both, at], out[both:, at]], axis=1))
    result = middle(jnp.concatenate(spectra, axis=0), weights, ins, outs, totals)
    for pair in range(plan.kstep // 2):
        columns = []
        for n in range(2):
            at = slice((2 * pair + n) * both, (2 * pair + n + 1) * both)
            columns.append(jnp.concatenate([result[at, :LANES], result[at, LANES:]], axis=0))
        out = dot(lat_back_ref[...], jnp.concatenate(columns, axis=1)) * plan.scale
        for n in range(2):
            k = step * plan.kstep + 2 * pair + n
            at = slice(n * LANES, (n + 1) * LANES)
            for kind in range(2):
                for order in range(2):
                    low = kind * both + order * slots
                    tall_refs[order][pl.ds(kind * plan.padwave + k, slots, stride=pitch), :] = out[
                        low : low + slots, at
                    ]

    @pl.when(step == pl.num_programs(0) - 1)
    def _():
        for ref, tall_ref in zip(back_refs, tall_refs):

            def move(h, _, ref=ref, tall_ref=tall_ref):
                row = pl.multiple_of(h * pitch, 8)
                to = pl.multiple_of(h * 2 * plan.padwave, 16)
                ref[pl.ds(to, 2 * plan.padwave), :] = tall_ref[pl.ds(row, 2 * plan.padwave), :].astype(bf16)
                return _

            lax.fori_loop(0, slots, move, 0, unroll=4)

        if totals:
            size = plan.size
            low, high = slice(0, size), slice(LANES, LANES + size)
            for n, total in enumerate(totals[:2]):
                base = 2 * size * n
                sums_ref[base : base + size] = total[low, :LANES] + total[high, LANES:]
                sums_ref[base + size : base + 2 * size] = total[low, LANES:] - total[high, :LANES]
            rows = [total[:, at] for total in totals[2:] for at in (slice(0, LANES), slice(LANES, None))]
            rows.append(jnp.zeros((sums_ref.shape[0] - 4 * size - 4, LANES), f32))
            sums_ref[4 * size :] = jnp.concatenate(rows, axis=0)


def sum_rows(plan):
    return -(-(4 * plan.size + 4) // 16) * 16


def wave_call(plan, middle, mine, other, tables, weights, streams_in, out_types, sums):
    consts = tables + weights
    part = pl.BlockSpec((2, plan.kstep * plan.slots, LANES), lambda s: (0, s, 0))
    stream = pl.BlockSpec((plan.kstep * HALVES * plan.slots, 2 * LANES), lambda s: (s, 0))
    sum_shapes = [(sum_rows(plan), LANES)] if sums else []
    total_shapes = [(2 * LANES, 2 * LANES)] * 2 + [(1, 2 * LANES)] * 2 if sums else []
    back = jax.ShapeDtypeStruct((plan.slots * 2 * plan.padwave, LANES), bf16)
    rows = plan.waves * HALVES * plan.slots
    return pl.pallas_call(
        functools.partial(wave_kernel, plan, middle, (len(streams_in), len(out_types), len(sum_shapes))),
        grid=(plan.waves // plan.kstep,),
        in_specs=[part] * 2 + [full(c.shape) for c in consts] + [stream] * len(streams_in),
        out_specs=[full(back.shape)] * 2 + [stream] * len(out_types) + [full(s) for s in sum_shapes],
        out_shape=[back] * 2
        + [jax.ShapeDtypeStruct((rows, 2 * LANES), t) for t in out_types]
        + [jax.ShapeDtypeStruct(s, f32) for s in sum_shapes],
        scratch_shapes=[pltpu.VMEM((plan.slots * odd_pitch(2 * plan.padwave), LANES), f32)] * 2
        + [pltpu.VMEM(v, f32) for v in total_shapes],
        compiler_params=params(48),
        cost_estimate=cost(20e9, 24e6),
    )(mine, other, *consts, *streams_in)


def back_kernel(plan, summed, mine_ref, other_ref, table_ref, *refs):
    g = pl.program_id(0)
    held_ref = refs[0] if summed else None
    send_ref = refs[1 if summed else 0]
    totals = refs[2:] if summed else ()
    kinds, size, pad = 2 * plan.padwave, plan.size, plan.padcol
    rows = pl.ds(pl.multiple_of(g * pad, 16), pad)

    if summed:

        @pl.when(g == 0)
        def _():
            for total in totals:
                total[...] = jnp.zeros_like(total)

    for lat in range(plan.lat):
        pieces = []
        for pair in range(GROUP // 2):
            columns = []
            for i in (2 * pair, 2 * pair + 1):
                at = pl.ds(pl.multiple_of((lat * plan.part + GROUP * g + i) * kinds, 16), kinds)
                columns.append(jnp.concatenate([mine_ref[at, :], other_ref[at, :]], axis=0))
            out = dot(table_ref[...], jnp.concatenate(columns, axis=1)).astype(bf16)
            pieces += [out[:, :size], out[:, LANES : LANES + size]]
        out = jnp.concatenate(pieces, axis=1)
        for lon in range(plan.lon):
            source = lon * plan.lat + lat
            value = out[lon * pad : (lon + 1) * pad]
            send_ref[source, rows, :] = value
            if summed:
                value = value.astype(f32)
                bump(totals[0], value * held_ref[source, rows, :].astype(f32))
                bump(totals[1], value)


def back_call(plan, mine, other, table, held=None):
    consts = (mine, other, table) + (() if held is None else (held,))
    shapes = [packet_shape(plan, plan.places)]
    if held is not None:
        shapes += [jax.ShapeDtypeStruct((1, plan.lanes), f32)] * 2
    return pl.pallas_call(
        functools.partial(back_kernel, plan, held is not None),
        grid=(plan.groups,),
        in_specs=[full(c.shape) for c in consts],
        out_specs=[full(v.shape) for v in shapes],
        out_shape=shapes,
        compiler_params=params(32),
        cost_estimate=cost(4e9, 8e6),
    )(*consts)


def forward_middle(freq, weights, ins, outs, totals):
    w_in_ref, w_out_ref, b_in_ref, b_out_ref = weights
    freq_ref, hid_ref, slope_ref = outs
    freq = freq.astype(bf16)
    freq_ref[...] = freq
    hid, slope = gelu_pair(dot(freq, w_in_ref[...]) + b_in_ref[...])
    hid = hid.astype(bf16)
    hid_ref[...] = hid
    slope_ref[...] = slope.astype(slope_ref.dtype)
    out = dot(hid, w_out_ref[...]) + b_out_ref[...]
    return (out - shrink_level * out * lax.rsqrt(out * out + shrink_level * shrink_level)).astype(bf16)


def backward_middle(grad_spec, weights, ins, outs, totals):
    w_in_ref, w_out_ref, b_in_ref, b_out_ref = weights
    freq_ref, hid_ref, slope_ref = ins
    in_sum_ref, out_sum_ref, in_bias_ref, out_bias_ref = totals
    hid = hid_ref[...]
    out = dot(hid, w_out_ref[...]) + b_out_ref[...]
    r = lax.rsqrt(out * out + shrink_level * shrink_level)
    grad_out = (grad_spec * (1.0 - shrink_level**3 * (r * r * r))).astype(bf16)
    out_sum_ref[...] += dot_tn(hid, grad_out)
    bump(out_bias_ref, grad_out.astype(f32))
    grad_pre = (dot_nt(grad_out, w_out_ref[...]) * slope_ref[...].astype(f32)).astype(bf16)
    in_sum_ref[...] += dot_tn(freq_ref[...], grad_pre)
    bump(in_bias_ref, grad_pre.astype(f32))
    return dot_nt(grad_pre, w_in_ref[...]).astype(bf16)


def block_matrix(plan, weight):
    pad = ((0, LANES - plan.size), (0, LANES - plan.size))
    real = jnp.pad(weight[0], pad)
    imag = jnp.pad(weight[1], pad)
    return jnp.concatenate(
        [jnp.concatenate([real, imag], axis=1), jnp.concatenate([-imag, real], axis=1)], axis=0
    )


def block_bias(plan, bias):
    return jnp.pad(bias.astype(f32), ((0, 0), (0, LANES - plan.size))).reshape(1, 2 * LANES)


FCHUNK = 512
PAIR = 2


def ffn_kernel(plan, hidden, kept, *refs):
    (
        meta_ref,
        frames_ref,
        cot_ref,
        recv_ref,
        other_ref,
        gain_one_ref,
        shift_one_ref,
        gain_two_ref,
        shift_two_ref,
        b_hidden_ref,
        b_out_ref,
        *weight_refs,
    ) = refs[:15]
    (
        second_ref,
        branch_grad_ref,
        hid_ref,
        pre_grad_ref,
        mixed_ref,
        send_ref,
        give_ref,
        grad_mixed_ref,
        gain_sum_ref,
        shift_sum_ref,
        out_bias_sum_ref,
        gain_one_sum_ref,
        shift_one_sum_ref,
        hidden_bias_sum_ref,
        filt_ref,
        keep_ref,
        branch_ref,
        grad_ref,
    ) = refs[15 + kept :]
    order, pair = pl.program_id(0), pl.program_id(1)
    d = meta_ref[6]
    half = jnp.where(order == 0, d, 1 - d)
    rows = [PAIR * pair + n for n in range(PAIR)]

    @pl.when((order == 0) & (pair == 0))
    def _():
        for ref in (
            gain_sum_ref,
            shift_sum_ref,
            out_bias_sum_ref,
            gain_one_sum_ref,
            shift_one_sum_ref,
            hidden_bias_sum_ref,
        ):
            ref[...] = jnp.zeros_like(ref)

    @pl.when((order == 0) & (pair == 0))
    def _():
        for n in range(GROUP):
            filt_ref[n] = join_blocks(plan, recv_ref, d * plan.blocks, n)

    @pl.when((order == 1) & (pair == 0))
    def _():
        for n in range(GROUP):
            filt_ref[n] = join_blocks(plan, other_ref, 0, n)

    def tile(load):
        return jnp.concatenate([load(i) for i in rows], axis=0)

    mask = tile(lambda i: row_mask(plan, meta_ref, half, i))
    inside = tile(lambda i: load_row(plan, frames_ref, half, i)).astype(f32) * mask
    xhat_one, _ = statistics(inside)
    normed = xhat_one * gain_one_ref[...] + shift_one_ref[...]
    mixed = tile(lambda i: filt_ref[i]).astype(f32) + normed + inside
    xhat, r = statistics(mixed)
    second = (xhat * gain_two_ref[...] + shift_two_ref[...]).astype(bf16)
    second_ref[...] = second
    grad_out = tile(lambda i: load_row(plan, cot_ref, half, i)).astype(f32) * mask
    grad_branch = grad_out.astype(bf16)
    branch_grad_ref[...] = grad_branch
    bump(out_bias_sum_ref, grad_branch.astype(f32))
    for c in range(hidden // FCHUNK):
        at = slice(c * FCHUNK, (c + 1) * FCHUNK)
        which, low = divmod(c * FCHUNK, hidden // 2)
        w_hidden = weight_refs[which][low : low + FCHUNK, :]
        w_out = weight_refs[2 + which][low : low + FCHUNK, :]
        hid, slope = gelu_pair(dot_nt(second, w_hidden) + b_hidden_ref[:, at])
        hid = hid.astype(bf16)
        hid_ref[:, at] = hid
        grad_pre = (dot_nt(grad_branch, w_out) * slope).astype(bf16)
        pre_grad_ref[:, at] = grad_pre
        hidden_bias_sum_ref[:, at] += jnp.sum(grad_pre.astype(f32), axis=0, keepdims=True)
        if c == 0:
            branch_ref[...] = dot(hid, w_out)
            grad_ref[...] = dot(grad_pre, w_hidden)
        else:
            branch_ref[...] += dot(hid, w_out)
            grad_ref[...] += dot(grad_pre, w_hidden)
    out = ((mixed + branch_ref[...] + b_out_ref[...]) * mask).astype(bf16)
    for n in range(PAIR):
        store_row(plan, mixed_ref, out[n * plan.packed : (n + 1) * plan.packed], half, rows[n])
    grad_second = grad_ref[...]
    bump(gain_sum_ref, grad_second * xhat)
    bump(shift_sum_ref, grad_second)
    grad_mixed = grad_out + norm_back(grad_second * gain_two_ref[...], xhat, r)
    grad_mixed_ref[0] = grad_mixed
    bump(gain_one_sum_ref, grad_mixed * xhat_one)
    bump(shift_one_sum_ref, grad_mixed)
    for n in range(PAIR):
        keep_ref[rows[n]] = grad_mixed[n * plan.packed : (n + 1) * plan.packed].astype(bf16)

    for core in range(2):

        @pl.when((order == 0) & (pair == GROUP // PAIR - 1) & (d == core))
        def _():
            split_blocks(plan, send_ref, core * plan.blocks, [keep_ref[n] for n in range(GROUP)])

    @pl.when((order == 1) & (pair == GROUP // PAIR - 1))
    def _():
        split_blocks(plan, give_ref, 0, [keep_ref[n] for n in range(GROUP)])


def ffn_call(plan, slot, meta, frames, cot, recv, other, consts, kept):
    hidden = consts[4].shape[1]
    pairs = GROUP // PAIR
    tiles = HALVES * pairs
    height = PAIR * plan.packed
    token = pl.BlockSpec((height, plan.channels), lambda n, i: (slot * tiles + n * pairs + i, 0))
    wide = pl.BlockSpec((height, hidden), lambda n, i: (slot * tiles + n * pairs + i, 0))
    sums = [(1, plan.channels)] * 5 + [(1, hidden)]
    kept_shapes = [
        jax.ShapeDtypeStruct((plan.micro * tiles * height, n), bf16)
        for n in (plan.channels, plan.channels, hidden, hidden)
    ]
    own_shapes = [tile_shape(plan), packet_shape(plan, plan.places), packet_shape(plan, plan.blocks)]
    return pl.pallas_call(
        functools.partial(ffn_kernel, plan, hidden, len(kept)),
        grid=(HALVES, pairs),
        in_specs=[SCALARS, tile_spec(plan, slot), tile_spec(plan, slot), full(recv.shape), full(other.shape)]
        + [full(c.shape) for c in consts]
        + [pl.BlockSpec(memory_space=pl.ANY)] * len(kept),
        out_specs=[token, token, wide, wide]
        + [full(v.shape) for v in own_shapes]
        + [pl.BlockSpec((1, height, plan.channels), lambda n, i: (n * pairs + i, 0, 0))]
        + [full(v) for v in sums],
        out_shape=kept_shapes
        + own_shapes
        + [jax.ShapeDtypeStruct((tiles, height, plan.channels), f32)]
        + [jax.ShapeDtypeStruct(v, f32) for v in sums],
        scratch_shapes=[
            pltpu.VMEM((GROUP, plan.packed, plan.channels), bf16),
            pltpu.VMEM((GROUP, plan.packed, plan.channels), bf16),
            pltpu.VMEM((height, plan.channels), f32),
            pltpu.VMEM((height, plan.channels), f32),
        ],
        input_output_aliases={15 + n: n for n in range(len(kept))},
        compiler_params=params(60),
        cost_estimate=cost(45e9, 60e6),
    )(meta, frames, cot, recv, other, *consts, *kept)


def weight_kernel(near, second_ref, branch_grad_ref, hid_ref, pre_grad_ref, own_ref, other_ref):
    sums = [dot_tn(pre_grad_ref[...], second_ref[...]), dot_tn(hid_ref[...], branch_grad_ref[...])]
    for ref, mine in ((own_ref, pl.program_id(0) < near), (other_ref, pl.program_id(0) >= near)):

        @pl.when(mine)
        def _():
            for n in range(2):
                ref[0, n] = sums[n].astype(bf16)


def weight_call(kept, block):
    second, branch_grad, hid, pre_grad = kept
    tokens, channels = second.shape
    wide = pl.BlockSpec((tokens, block), lambda n: (0, n))
    near = hid.shape[1] // block // 2
    shape = (1, 2, block, channels)
    return pl.pallas_call(
        functools.partial(weight_kernel, near),
        grid=(2 * near,),
        in_specs=[full(second.shape), full(second.shape), wide, wide],
        out_specs=[
            pl.BlockSpec(shape, lambda n: (jnp.minimum(n, near - 1), 0, 0, 0)),
            pl.BlockSpec(shape, lambda n: (jnp.maximum(n - near, 0), 0, 0, 0)),
        ],
        out_shape=[jax.ShapeDtypeStruct((near,) + shape[1:], bf16)] * 2,
        compiler_params=params(48),
        cost_estimate=cost(22e9, 46e6),
    )(second, branch_grad, hid, pre_grad)


def last_kernel(plan, meta_ref, frames_ref, recv_ref, other_ref, grad_mixed_ref, gain_ref, out_ref):
    d = meta_ref[6]
    for n, ref, first in ((0, recv_ref, d * plan.blocks), (1, other_ref, 0)):
        half = d if n == 0 else 1 - d
        for i in range(GROUP):
            mask = row_mask(plan, meta_ref, half, i)
            xhat, r = statistics(load_row(plan, frames_ref, half, i).astype(f32) * mask)
            at = slice((i % PAIR) * plan.packed, (i % PAIR + 1) * plan.packed)
            grad_mixed = grad_mixed_ref[n * (GROUP // PAIR) + i // PAIR, at, :]
            grad_normed = join_blocks(plan, ref, first, i).astype(f32) + grad_mixed
            grad_inside = grad_mixed + norm_back(grad_normed * gain_ref[...], xhat, r)
            store_row(plan, out_ref, (grad_inside * mask).astype(bf16), half, i)


def last_call(plan, slot, meta, frames, recv, other, grad_mixed, gain):
    shape = tile_shape(plan)
    return pl.pallas_call(
        functools.partial(last_kernel, plan),
        grid=(1,),
        in_specs=[SCALARS, tile_spec(plan, slot)] + [full(v.shape) for v in (recv, other, grad_mixed, gain)],
        out_specs=full(shape.shape),
        out_shape=shape,
        compiler_params=params(40),
        cost_estimate=cost(8e9, 10e6),
    )(meta, frames, recv, other, grad_mixed, gain)


AXES = ("dp", "lon", "lat")


def exchange(values):
    return lax.all_to_all(values, ("lon", "lat"), 0, 0, tiled=True)


def swap(value, axis, bit):
    count = lax.axis_size(axis)
    return lax.ppermute(value, axis, [(n, n ^ bit) for n in range(count)])


def after(value, *others):
    return lax.optimization_barrier((value,) + others)[0]


def near(value, axis):
    return [value] + [swap(value, axis, d) for d in range(1, lax.axis_size(axis))]


def add(terms):
    return sum(v.astype(f32) for v in terms)


def near_to_place(value, axis, dim):
    count = lax.axis_size(axis)
    shape = value.shape
    bit = 1
    while bit < count:
        split = value.reshape(shape[:dim] + (count // (2 * bit), 2, bit) + shape[dim + 1 :])
        turned = jnp.flip(split, dim + 1)
        value = jnp.where((lax.axis_index(axis) & bit) == 0, split, turned).reshape(shape)
        bit *= 2
    return value


def sum_over(value, axis):
    bit = 1
    while bit < lax.axis_size(axis):
        value = value + swap(value, axis, bit)
        bit *= 2
    return value


def collect(value, axis, bits):
    for bit in bits:
        other = swap(value, axis, bit)
        low = (lax.axis_index(axis) & bit) == 0
        value = jnp.concatenate([jnp.where(low, value, other), jnp.where(low, other, value)], axis=0)
    return value


def body(
    frames,
    regions,
    cotangent,
    first_gain,
    first_shift,
    inner_weight,
    inner_bias,
    outer_weight,
    outer_bias,
    second_gain,
    second_shift,
    hidden_weight,
    hidden_bias,
    output_weight,
    output_bias,
):
    dp, lon, lat = (lax.axis_size(a) for a in AXES)
    dp_place, lon_place, lat_place = (lax.axis_index(a) for a in AXES)
    core = dp_place % 2
    micro, rows, cols, channels = frames.shape
    blocks = inner_weight.shape[0]
    plan = Plan(micro, rows, cols, channels, blocks, lat, lon)
    size = plan.size
    own_block = (lon_place * lat + lat_place) % blocks
    hidden_rows = hidden_weight.shape[0]
    hidden = hidden_rows * dp * lon * lat

    origin = jnp.stack([lat_place * rows, lon_place * cols, core]).astype(jnp.int32)
    metas = [jnp.concatenate([regions[s], origin]) for s in range(micro)]
    lon_table, lon_back_table = (jnp.asarray(t) for t in lon_tables(plan))
    pick = lambda t: lax.dynamic_index_in_dim(t, core, 0, keepdims=False)
    lon_back_table = pick(lon_back_table)
    tables = tuple(pick(jnp.asarray(t)) for t in lat_tables(plan))

    def row(v):
        return v.astype(f32).reshape(1, -1)

    def own(v):
        return lax.dynamic_index_in_dim(v, own_block, 0, keepdims=False)

    def padded(v):
        return jnp.pad(v, ((0, 0), (0, HALVES * plan.part - rows), (0, plan.padcol - cols), (0, 0)))

    def whole(parts):
        return jnp.stack(parts)[:, :rows, :cols]

    def join(send, give):
        return lax.dynamic_update_slice_in_dim(send, swap(give, "dp", 1), (1 - core) * blocks, 0)

    def other(received):
        return swap(lax.dynamic_slice_in_dim(received, (1 - core) * blocks, blocks, 0), "dp", 1)

    frame_tiles = padded(frames)
    cot_tiles = padded(cotangent)
    spectral_weights = (
        block_matrix(plan, own(inner_weight)),
        block_matrix(plan, own(outer_weight)),
        block_bias(plan, own(inner_bias)),
        block_bias(plan, own(outer_bias)),
    )
    slots = range(micro)

    bias_row = jnp.pad(hidden_bias.reshape(1, hidden_rows), ((0, 7), (0, channels - hidden_rows)))
    gathered = jnp.concatenate([hidden_weight, output_weight, bias_row], axis=0)
    metas[0] = after(metas[0], gathered)
    near_lat = jnp.stack(near(gathered, "lat"))
    gathered = lax.all_gather(near_lat, "lon", axis=0)
    gathered = gathered.reshape(lon * lat, -1, channels)
    done = (near_lat,)

    turn = []

    def queue(value):
        return after(value, *turn)

    def ran(output):
        turn[:] = [output]

    normed, sends = [], []
    for s in slots:
        send, give = first_call(plan, s, queue(metas[s]), frame_tiles, row(first_gain), row(first_shift))
        sends.append(join(send, give))
        ran(sends[-1])
        normed.append(exchange(after(sends[s], *done)))
        done = (normed[-1],)

    def start_waves(s, received):
        mine, give = lon_call(plan, metas[s], queue(received), lon_table)
        ran(mine)
        return mine, swap(give, "dp", 1)

    def waves_of(mine, other, middle, *args):
        mine, give, *rest = wave_call(plan, middle, queue(mine), other, tables, spectral_weights, *args)
        ran(mine)
        return (mine, swap(give, "dp", 1)), rest

    def field_of(mine, other, held=None):
        out = back_call(plan, queue(mine), other, lon_back_table, held)
        ran(out[0])
        return out

    def feed_forward_inputs(gathered):
        half = hidden // 2

        def gathered_rows(low):
            parts = near(gathered[:, low : low + hidden_rows].reshape(-1, channels), "dp")
            if dp == 2:
                return parts
            parts = jnp.concatenate(parts, axis=0)
            return [parts[:half], parts[half:]]

        b_hidden = jnp.stack(near(gathered[:, 2 * hidden_rows, :hidden_rows], "dp"))
        b_hidden = b_hidden.astype(f32).reshape(1, hidden)
        return (
            row(first_gain),
            row(first_shift),
            row(second_gain),
            row(second_shift),
            b_hidden,
            row(output_bias),
            *gathered_rows(0),
            *gathered_rows(hidden_rows),
        )

    filtered, kept_waves = [], []
    for s in slots:
        pair = start_waves(s, normed[s])
        if s + 1 == micro:
            gathered = after(gathered, pair[0])
            consts = feed_forward_inputs(gathered)
        pair, waves = waves_of(*pair, forward_middle, (), (bf16, bf16, bf16), False)
        kept_waves.append(waves)
        before = done + consts + (cot_tiles,) if s + 1 == micro else ()
        (send,) = field_of(after(pair[0], *before), pair[1])
        filtered.append(exchange(after(send, *done)))
        done = (filtered[-1],)

    kept = ()
    mixed, grad_mixed, grads, token_sums = [], [], [], []
    for s in slots:
        out = ffn_call(
            plan, s, queue(metas[s]), frame_tiles, cot_tiles, filtered[s], other(filtered[s]), consts, kept
        )
        kept = tuple(out[:4])
        mixed.append(out[4])
        joined = join(out[5], out[6])
        ran(joined)
        grads.append(exchange(after(joined, *done)))
        done = (grads[-1],)
        grad_mixed.append(out[7])
        token_sums.append(out[8:])
    token_sums = [sum(v) for v in zip(*token_sums)]
    hidden_bias_sum = token_sums.pop().reshape(dp, lon, lat, hidden_rows)
    hidden_bias_sum = near_to_place(near_to_place(hidden_bias_sum, "dp", 0), "lat", 2)

    block = 3 * LANES
    wave_sums, field_sums, sends = [], [], []
    parts = weight_call((queue(kept[0]),) + kept[1:], block)
    ran(parts[0])
    pair = start_waves(0, after(grads[0], *done))
    for s in slots:
        pair, waves = waves_of(*pair, backward_middle, kept_waves[s], (), True)
        wave_sums.append(waves)
        following = start_waves(s + 1, grads[s + 1]) if s + 1 < micro else None
        send, *sums = field_of(*pair, normed[s])
        field_sums.append(sums)
        sends.append(send)
        pair = following
    if dp == 2 and parts[0].shape[0] == lon:
        terms = [parts[0], after(swap(parts[1], "dp", 1), sends[0])]
    else:
        parts = jnp.concatenate(parts, axis=0).transpose(1, 0, 2, 3)
        parts = parts.reshape(2, dp, lon, lat * hidden_rows, channels).transpose(1, 2, 0, 3, 4)
        terms = [parts[0]] + [swap(parts[n], "dp", n) for n in range(1, dp)]
    own_part = add(terms).astype(bf16)
    lat_part = lax.psum_scatter(own_part.reshape(lon, -1, channels), "lon", scatter_dimension=0)
    lat_part = lat_part.reshape(2, lat, hidden_rows, channels)
    ffn_grads = add([lat_part[:, 0]] + [swap(lat_part[:, n], "lat", n) for n in range(1, lat)])
    product_sum, plain_sum = (sum(v) for v in zip(*field_sums))

    plain = jnp.sum(plain_sum.reshape(GROUP, size), axis=0)
    product = jnp.sum(product_sum.reshape(GROUP, size), axis=0)
    own_shift = own(first_shift.astype(f32).reshape(blocks, size))
    own_gain = own(first_gain.astype(f32).reshape(blocks, size))

    block_sums = sum(v[0] for v in wave_sums)
    bit = 2
    while bit < dp:
        block_sums = block_sums + swap(block_sums, "dp", bit)
        bit *= 2
    half_rows = block_sums.shape[0] // 2
    part_of = lambda n: lax.dynamic_slice_in_dim(block_sums, n * half_rows, half_rows, 0)
    block_sums = part_of(core) + swap(part_of(1 - core), "dp", 1)
    lon_blocks = blocks // lat
    bit = lon_blocks
    while bit < lon:
        block_sums = block_sums + swap(block_sums, "lon", bit)
        bit *= 2
    all_sums = block_sums[None]
    some_sums = all_sums
    all_sums = collect(all_sums, "lat", [1 << n for n in range(lat.bit_length() - 1)])
    all_sums = collect(all_sums, "lon", [1 << n for n in range(lon_blocks.bit_length() - 1)])
    all_sums = collect(all_sums[None], "dp", [1])
    all_sums = jnp.concatenate([all_sums[0], all_sums[1]], axis=1)
    all_sums = all_sums[:, :, :size]
    inner_grad = all_sums[:, : 2 * size].reshape(blocks, 2, size, size)
    outer_grad = all_sums[:, 2 * size : 4 * size].reshape(blocks, 2, size, size)
    base = 4 * size
    inner_bias_grad = all_sums[:, base : base + 2]
    outer_bias_grad = all_sums[:, base + 2 : base + 4]

    back, frame_grads = [], []
    for s in slots:
        last = s + 1 == micro
        back.append(exchange(after(sends[s], *done, *((some_sums,) if last else ()))))
        done = (back[-1],)
        if last:
            ran(ffn_grads)
        frame_grads.append(
            last_call(plan, s, queue(metas[s]), frame_tiles, back[s], other(back[s]), grad_mixed[s], row(first_gain))
        )
        ran(frame_grads[-1])

    def spread(value):
        return lax.dynamic_update_slice_in_dim(jnp.zeros((blocks, size), f32), value[None], own_block, 0)

    small = token_sums + [
        hidden_bias_sum,
        spread((product - own_shift * plain) / own_gain),
        spread(plain),
    ]
    small = jnp.concatenate([v.reshape(-1) for v in small]).reshape(-1, LANES)
    for axis in AXES:
        small = sum_over(small, axis)
    small = small.reshape(-1)
    second_gain_grad, second_shift_grad, output_bias_grad, gain_part, shift_part = (
        small[n * channels : (n + 1) * channels] for n in range(5)
    )
    order = lax.axis_index(AXES)
    hidden_bias_grad = lax.dynamic_slice_in_dim(small[5 * channels :], order * hidden_rows, hidden_rows, 0)
    base = 5 * channels + hidden
    first_gain_grad = gain_part + small[base : base + channels]
    first_shift_grad = shift_part + small[base + channels :]
    return (
        whole(mixed),
        whole(frame_grads),
        first_gain_grad,
        first_shift_grad,
        inner_grad,
        inner_bias_grad,
        outer_grad,
        outer_bias_grad,
        second_gain_grad,
        second_shift_grad,
        ffn_grads[0],
        hidden_bias_grad,
        ffn_grads[1],
        output_bias_grad,
    )


def solution(mesh):
    field = P("dp", "lat", "lon", None)
    rows = P(AXES, None)
    return jax.shard_map(
        body,
        mesh=mesh,
        in_specs=(field, P("dp", None), field) + (P(),) * 8 + (rows, P(AXES), rows, P()),
        out_specs=(field, field) + (P(),) * 8 + (rows, P(AXES), rows, P()),
        check_vma=False,
    )
```

time: 859 us -> 625 us (0.73)
  the two profiles are of different devices: /device:TPU:0 before, /device:TPU:10 now
where the time goes in v2:
time: 625 us; the launch traced here: 613 us
  Pallas kernels  236 us (38%)
  waiting for transfers between devices  150 us (24%)
  starting transfers between devices  92.2 us (15%)
  local copies, waits for them, and re-layouts  90.5 us (14%)
  other arithmetic  29.1 us (5%)
  between operations  15.4 us (2%)
    ppermute x37, waiting for transfers between devices, swap(): return lax.ppermute(value, axis, [(n, n ^ bit) for n in range(count)])  92 us
    pallas_call x2, Pallas kernels, ffn_call(): pl.pallas_call(functools.partial(ffn_kernel, plan, hidden, len(kept)), gr...  85.6 us
    pallas_call x4, Pallas kernels, wave_call(): pl.pallas_call(functools.partial(wave_kernel, plan, middle, (len(streams_...  69.7 us
    all_to_all x8, starting transfers between devices, exchange(): return lax.all_to_all(values, ('lon', 'lat'), 0, 0, tiled=True)  60.9 us
    all_to_all x8, waiting for transfers between devices, exchange(): return lax.all_to_all(values, ('lon', 'lat'), 0, 0, tiled=True)  57.8 us
    unnamed x173, local copies, waits for them, and re-layouts  52.8 us
    ppermute x37, starting transfers between devices, swap(): return lax.ppermute(value, axis, [(n, n ^ bit) for n in range(count)])  31 us
    pallas_call x1, Pallas kernels, weight_call(): pl.pallas_call(functools.partial(weight_kernel, near), grid=(2 * near,),...  29.1 us
  transfers between devices with their start and end apart: 47, of which 24 were waited for; matrix products, arithmetic and copies ran while one was open for 11% of the time, Pallas kernels for 36%

profile of v2, /device:TPU:10, one launch (start us, length us, event | category | flops | bytes accessed | tf_op | source)
XLA Modules:
  0.0 613.5 jit_solution(4643952139565947258)
XLA Ops:
  21.9 10.7 %collective-permute-done.2 = bf16[200,768]{1,0:T(8,128)(2,1)} collective-permute-done((bf16[200,768]{1,0:T(8,128)(2,1)}, bf16[200,768]{1,0:T(8,128)(2,1)}, u32[]{:S(2)}, u32[]{:S(2)}) %collective-permute-start.2) | collective-permute-done | bytes 307232 | tf_op jit(solution)/shard_map/ppermute | solution.py:705
  32.5 10.1 %collective-permute-done.3 = bf16[200,768]{1,0:T(8,128)(2,1)} collective-permute-done((bf16[200,768]{1,0:T(8,128)(2,1)}, bf16[200,768]{1,0:T(8,128)(2,1)}, u32[]{:S(2)}, u32[]{:S(2)}) %collective-permute-start.3) | collective-permute-done | bytes 307232 | tf_op jit(solution)/shard_map/ppermute | solution.py:705
  42.6 6.8 %collective-permute-done.4 = bf16[200,768]{1,0:T(8,128)(2,1)} collective-permute-done((bf16[200,768]{1,0:T(8,128)(2,1)}, bf16[200,768]{1,0:T(8,128)(2,1)}, u32[]{:S(2)}, u32[]{:S(2)}) %collective-permute-start.4) | collective-permute-done | bytes 307232 | tf_op jit(solution)/shard_map/ppermute | solution.py:705
  69.3 29.0 %all-to-all-done.recv_ref.refs_0_ = bf16[16,144,384]{2,1,0:T(8,128)(2,1)} async-done(((bf16[16,144,384]{2,1,0:T(8,128)(2,1)}), bf16[16,144,384]{2,1,0:T(8,128)(2,1)}, u32[]{:S(2)}, u32[]{:S(2)}) %all-to-all-start) | async-done | bytes 1769504 | tf_op jit(solution)/shard_map/all_to_all | solution.py:700
  106.5 8.1 %all-to-all-start.1 = ((bf16[16,144,384]{2,1,0:T(8,128)(2,1)}), bf16[16,144,384]{2,1,0:T(8,128)(2,1)S(1)}, u32[]{:S(2)}, u32[]{:S(2)}) async-start(bf16[16,144,384]{2,1,0:T(8,128)(2,1)} %constant_dynamic-update-slice_fusion.2), calls=%async_computation.1 | async-start | bytes 3538944 | tf_op jit(solution)/shard_map/all_to_all | solution.py:700
  118.0 16.8 %shard_map.293 = (bf16[9216,128]{1,0:T(8,128)(2,1)}, bf16[9216,128]{1,0:T(8,128)(2,1)}, bf16[8640,256]{1,0:T(8,128)(2,1)}, bf16[8640,256]{1,0:T(8,128)(2,1)}, bf16[8640,256]{1,0:T(8,128)(2,1)}) custom-call(bf16[2,4320,128]{2,1,0:T(8,128)(2,1)S(1)} %copy-done.31, bf16[2,4320,128]{2,1,0:T(8,128)(2,1)} %collective-permute-done.5.refs_1_, ...), custom_call_target="tpu_custom_call" | custom-call | flops 1000000000 | bytes 1200000 | tf_op jit(solution)/shard_map/pallas_call | solution.py:370
  144.4 11.5 %all-to-all-done.1.recv_ref.refs_0_ = bf16[16,144,384]{2,1,0:T(8,128)(2,1)S(1)} async-done(((bf16[16,144,384]{2,1,0:T(8,128)(2,1)}), bf16[16,144,384]{2,1,0:T(8,128)(2,1)S(1)}, u32[]{:S(2)}, u32[]{:S(2)}) %all-to-all-start.1) | async-done | bytes 1769504 | tf_op jit(solution)/shard_map/all_to_all | solution.py:700
  162.3 9.8 %all-to-all-start.2 = ((bf16[16,144,384]{2,1,0:T(8,128)(2,1)}), bf16[16,144,384]{2,1,0:T(8,128)(2,1)}, u32[]{:S(2)}, u32[]{:S(2)}) async-start(bf16[16,144,384]{2,1,0:T(8,128)(2,1)} %shard_map.294), calls=%async_computation.2 | async-start | bytes 3538944 | tf_op jit(solution)/shard_map/all_to_all | solution.py:700
  177.9 16.8 %shard_map.296 = (bf16[9216,128]{1,0:T(8,128)(2,1)}, bf16[9216,128]{1,0:T(8,128)(2,1)}, bf16[8640,256]{1,0:T(8,128)(2,1)}, bf16[8640,256]{1,0:T(8,128)(2,1)}, bf16[8640,256]{1,0:T(8,128)(2,1)}) custom-call(bf16[2,4320,128]{2,1,0:T(8,128)(2,1)S(1)} %copy-done.33, bf16[2,4320,128]{2,1,0:T(8,128)(2,1)} %collective-permute-done.7.refs_1_, ...), custom_call_target="tpu_custom_call" | custom-call | flops 1000000000 | bytes 1200000 | tf_op jit(solution)/shard_map/pallas_call | solution.py:370
  201.6 9.8 %all-to-all-done.2.refs_3_ = bf16[16,144,384]{2,1,0:T(8,128)(2,1)} async-done(((bf16[16,144,384]{2,1,0:T(8,128)(2,1)}), bf16[16,144,384]{2,1,0:T(8,128)(2,1)}, u32[]{:S(2)}, u32[]{:S(2)}) %all-to-all-start.2) | async-done | bytes 1769504 | tf_op jit(solution)/shard_map/all_to_all | solution.py:700
  218.0 8.8 %all-to-all-start.3 = ((bf16[16,144,384]{2,1,0:T(8,128)(2,1)}), bf16[16,144,384]{2,1,0:T(8,128)(2,1)S(1)}, u32[]{:S(2)}, u32[]{:S(2)}) async-start(bf16[16,144,384]{2,1,0:T(8,128)(2,1)} %shard_map.297), calls=%async_computation.3 | async-start | bytes 3538944 | tf_op jit(solution)/shard_map/all_to_all | solution.py:700
  230.7 42.8 %shard_map.298 = (bf16[2304,768]{1,0:T(8,128)(2,1)}, bf16[2304,768]{1,0:T(8,128)(2,1)}, bf16[2304,3072]{1,0:T(8,128)(2,1)}, bf16[2304,3072]{1,0:T(8,128)(2,1)}, ...) custom-call(s32[7]{0:T(128)} %copy-done.45, ...), custom_call_target="tpu_custom_call" | custom-call | flops 2249999872 | bytes 3000000 | tf_op jit(solution)/shard_map/pallas_call | solution.py:613
  278.4 7.5 %all-to-all-start.4 = ((bf16[16,144,384]{2,1,0:T(8,128)(2,1)}), bf16[16,144,384]{2,1,0:T(8,128)(2,1)S(1)}, u32[]{:S(2)}, u32[]{:S(2)}) async-start(bf16[16,144,384]{2,1,0:T(8,128)(2,1)} %constant_dynamic-update-slice_fusion.1), calls=%async_computation.4 | async-start | bytes 3538944 | tf_op jit(solution)/shard_map/all_to_all | solution.py:700
  290.6 42.8 %shard_map.299 = (bf16[2304,768]{1,0:T(8,128)(2,1)}, bf16[2304,768]{1,0:T(8,128)(2,1)}, bf16[2304,3072]{1,0:T(8,128)(2,1)}, bf16[2304,3072]{1,0:T(8,128)(2,1)}, ...) custom-call(s32[7]{0:T(128)} %copy-done.47, ...), custom_call_target="tpu_custom_call", output_to_operand_aliasing={{0}: (15, {}), {1}: (16, {}), {2}: (17, {}), {3}: (18, {})} | custom-call | flops 2249999872 | bytes 3000000 | tf_op jit(solution)/shard_map/pallas_call | solution.py:613
  337.1 6.9 %all-to-all-start.5 = ((bf16[16,144,384]{2,1,0:T(8,128)(2,1)}), bf16[16,144,384]{2,1,0:T(8,128)(2,1)}, u32[]{:S(2)}, u32[]{:S(2)}) async-start(bf16[16,144,384]{2,1,0:T(8,128)(2,1)} %constant_dynamic-update-slice_fusion), calls=%async_computation.5 | async-start | bytes 3538944 | tf_op jit(solution)/shard_map/all_to_all | solution.py:700
  346.3 29.1 %shard_map.300 = (bf16[4,2,384,768]{3,2,1,0:T(8,128)(2,1)}, bf16[4,2,384,768]{3,2,1,0:T(8,128)(2,1)}) custom-call(bf16[2304,768]{1,0:T(8,128)(2,1)S(1)} %copy-done.2, bf16[2304,768]{1,0:T(8,128)(2,1)} %get-tuple-element.148.branch_grad_ref, bf16[2304,3072]{1,0:T(8,128)(2,1)} %get-tuple-element.149.hid_ref, bf16[2304,3072]{1,0:T(8,128)(2,1)} %get-tuple-element.150.pre_grad_ref), custom_call_target="tpu_custom_call" | custom-call | flops 1100000000 | bytes 2300000 | tf_op jit(solution)/shard_map/pallas_call | solution.py:655
  375.4 7.5 %all-to-all-done.5.recv_ref = bf16[16,144,384]{2,1,0:T(8,128)(2,1)} async-done(((bf16[16,144,384]{2,1,0:T(8,128)(2,1)}), bf16[16,144,384]{2,1,0:T(8,128)(2,1)}, u32[]{:S(2)}, u32[]{:S(2)}) %all-to-all-start.5) | async-done | bytes 1769504 | tf_op jit(solution)/shard_map/all_to_all | solution.py:700
  395.5 18.0 %shard_map.302 = (bf16[9216,128]{1,0:T(8,128)(2,1)}, bf16[9216,128]{1,0:T(8,128)(2,1)}, f32[400,128]{1,0:T(8,128)S(1)}) custom-call(bf16[2,4320,128]{2,1,0:T(8,128)(2,1)S(1)} %get-tuple-element.153.refs_0_, bf16[2,4320,128]{2,1,0:T(8,128)(2,1)S(1)} %collective-permute-done.16.refs_1_, bf16[192,192]{1,0:T(8,128)(2,1)S(1)} %copy-done.24, ...), custom_call_target="tpu_custom_call" | custom-call | flops 1000000000 | bytes 1200000 | tf_op jit(solution)/shard_map/pallas_call | solution.py:370
  425.6 6.4 %add_convert_fusion = bf16[4,2,384,768]{3,2,1,0:T(8,128)(2,1)} fusion(bf16[4,2,384,768]{3,2,1,0:T(8,128)(2,1)} %collective-permute-done.21, bf16[4,2,384,768]{3,2,1,0:T(8,128)(2,1)S(1)} %copy-done.60), kind=kLoop, calls=%fused_computation | loop fusion | flops 9437184 | bytes 14155776 | tf_op jit(solution)/shard_map/convert_element_type | solution.py:923
  432.5 8.2 %all-to-all-start.6 = ((bf16[16,144,384]{2,1,0:T(8,128)(2,1)}), bf16[16,144,384]{2,1,0:T(8,128)(2,1)S(1)}, u32[]{:S(2)}, u32[]{:S(2)}) async-start(bf16[16,144,384]{2,1,0:T(8,128)(2,1)} %copy-done.37), calls=%async_computation.6 | async-start | bytes 3538944 | tf_op jit(solution)/shard_map/all_to_all | solution.py:700
  451.4 18.1 %shard_map.305 = (bf16[9216,128]{1,0:T(8,128)(2,1)}, bf16[9216,128]{1,0:T(8,128)(2,1)}, f32[400,128]{1,0:T(8,128)S(1)}) custom-call(bf16[2,4320,128]{2,1,0:T(8,128)(2,1)S(1)} %copy-done.35, bf16[2,4320,128]{2,1,0:T(8,128)(2,1)} %collective-permute-done.18.refs_1_, bf16[192,192]{1,0:T(8,128)(2,1)S(1)} %copy-done.25, bf16[192,192]{1,0:T(8,128)(2,1)S(1)} %copy-done.22, ...), custom_call_target="tpu_custom_call" | custom-call | flops 1000000000 | bytes 1200000 | tf_op jit(solution)/shard_map/pallas_call | solution.py:370
  515.9 12.1 %collective-permute-done.35 = f32[4,200,128]{2,1,0:T(8,128)S(1)} collective-permute-done((f32[4,200,128]{2,1,0:T(8,128)S(1)}, f32[4,200,128]{2,1,0:T(8,128)S(1)}, u32[]{:S(2)}, u32[]{:S(2)}) %collective-permute-start.35) | collective-permute-done | bytes 409632 | tf_op jit(solution)/shard_map/ppermute | solution.py:705
  578.2 9.9 %collective-permute-done.23 = bf16[2,96,768]{2,1,0:T(8,128)(2,1)S(1)} collective-permute-done((bf16[2,96,768]{2,1,0:T(8,128)(2,1)S(1)}, bf16[2,96,768]{2,1,0:T(8,128)(2,1)S(1)}, u32[]{:S(2)}, u32[]{:S(2)}) %collective-permute-start.23) | collective-permute-done | bytes 294944 | tf_op jit(solution)/shard_map/ppermute | solution.py:705
  588.0 6.9 %collective-permute-done.24 = bf16[2,96,768]{2,1,0:T(8,128)(2,1)S(1)} collective-permute-done((bf16[2,96,768]{2,1,0:T(8,128)(2,1)S(1)}, bf16[2,96,768]{2,1,0:T(8,128)(2,1)S(1)}, u32[]{:S(2)}, u32[]{:S(2)}) %collective-permute-start.24) | collective-permute-done | bytes 294944 | tf_op jit(solution)/shard_map/ppermute | solution.py:705
  (357 shorter events, 243.9 us)
Async XLA Ops:
  18.4 33.5 %collective-permute-start = (bf16[8,144,384]{2,1,0:T(8,128)(2,1)}, bf16[8,144,384]{2,1,0:T(8,128)(2,1)}, u32[]{:S(2)}, u32[]{:S(2)}) collective-permute-start(bf16[8,144,384]{2,1,0:T(8,128)(2,1)} %get-tuple-element.108), channel_id=1, source_target_pairs={{0,16},{16,0},{1,17},{17,1},{2,18},{18,2},{3,19},{19,3},{4,20},{20... | collective-permute-start | bytes 2654216 | tf_op jit(solution)/shard_map/ppermute | solution.py:705
  18.8 23.7 %collective-permute-start.3 = (bf16[200,768]{1,0:T(8,128)(2,1)}, bf16[200,768]{1,0:T(8,128)(2,1)}, u32[]{:S(2)}, u32[]{:S(2)}) collective-permute-start(bf16[200,768]{1,0:T(8,128)(2,1)} %get-tuple-element.278), channel_id=1, source_target_pairs={{0,2},{1,3},{2,0},{3,1},{4,6},{5,7},{6,4},{7,5},{8,10},{9,11},{10,... | collective-permute-start | bytes 921608 | tf_op jit(solution)/shard_map/ppermute | solution.py:705
  21.4 28.0 %collective-permute-start.4 = (bf16[200,768]{1,0:T(8,128)(2,1)}, bf16[200,768]{1,0:T(8,128)(2,1)}, u32[]{:S(2)}, u32[]{:S(2)}) collective-permute-start(bf16[200,768]{1,0:T(8,128)(2,1)} %get-tuple-element.278), channel_id=1, source_target_pairs={{0,3},{1,2},{2,1},{3,0},{4,7},{5,6},{6,5},{7,4},{8,11},{9,10},{10,... | collective-permute-start | bytes 921608 | tf_op jit(solution)/shard_map/ppermute | solution.py:705
  54.0 44.3 %all-to-all-start = ((bf16[16,144,384]{2,1,0:T(8,128)(2,1)}), bf16[16,144,384]{2,1,0:T(8,128)(2,1)}, u32[]{:S(2)}, u32[]{:S(2)}) async-start(bf16[16,144,384]{2,1,0:T(8,128)(2,1)} %constant_dynamic-update-slice_fusion.3), calls=%async_computation | async-start | bytes 3538944 | tf_op jit(solution)/shard_map/all_to_all | solution.py:700
  60.2 112.0 %all-gather.3.cloned.1.call-start = ((), (), s32[]{:S(2)}) async-start(), calls=%async_computation.9 | async-start | bytes 6144000 | tf_op jit(solution)/shard_map/all_gather | solution.py:815
  106.5 49.3 %all-to-all-start.1 = ((bf16[16,144,384]{2,1,0:T(8,128)(2,1)}), bf16[16,144,384]{2,1,0:T(8,128)(2,1)S(1)}, u32[]{:S(2)}, u32[]{:S(2)}) async-start(bf16[16,144,384]{2,1,0:T(8,128)(2,1)} %constant_dynamic-update-slice_fusion.2), calls=%async_computation.1 | async-start | bytes 3538944 | tf_op jit(solution)/shard_map/all_to_all | solution.py:700
  162.3 15.5 %collective-permute-start.7 = (bf16[2,4320,128]{2,1,0:T(8,128)(2,1)}, bf16[2,4320,128]{2,1,0:T(8,128)(2,1)}, u32[]{:S(2)}, u32[]{:S(2)}) collective-permute-start(bf16[2,4320,128]{2,1,0:T(8,128)(2,1)} %get-tuple-element.123), channel_id=1, source_target_pairs={{0,16},{16,0},{1,17},{17,1},{2,18},{18,2},{3,19},{19,3},{4,20},{20... | collective-permute-start | bytes 6635528 | tf_op jit(solution)/shard_map/ppermute | solution.py:705
  162.3 49.1 %all-to-all-start.2 = ((bf16[16,144,384]{2,1,0:T(8,128)(2,1)}), bf16[16,144,384]{2,1,0:T(8,128)(2,1)}, u32[]{:S(2)}, u32[]{:S(2)}) async-start(bf16[16,144,384]{2,1,0:T(8,128)(2,1)} %shard_map.294), calls=%async_computation.2 | async-start | bytes 3538944 | tf_op jit(solution)/shard_map/all_to_all | solution.py:700
  177.3 24.2 %collective-permute-start.10 = (bf16[1536,768]{1,0:T(8,128)(2,1)}, bf16[1536,768]{1,0:T(8,128)(2,1)}, u32[]{:S(2)}, u32[]{:S(2)}) collective-permute-start(bf16[1536,768]{1,0:T(8,128)(2,1)} %bitcast.25.refs_13_), channel_id=1, source_target_pairs={{0,16},{16,0},{1,17},{17,1},{2,18},{18,2},{3,19},{19,3},{4,20},{20... | collective-permute-start | bytes 7077896 | tf_op jit(solution)/shard_map/ppermute | solution.py:705
  177.6 24.0 %collective-permute-start.9 = (bf16[1536,768]{1,0:T(8,128)(2,1)}, bf16[1536,768]{1,0:T(8,128)(2,1)}, u32[]{:S(2)}, u32[]{:S(2)}) collective-permute-start(bf16[1536,768]{1,0:T(8,128)(2,1)} %bitcast.24.refs_11_), channel_id=1, source_target_pairs={{0,16},{16,0},{1,17},{17,1},{2,18},{18,2},{3,19},{19,3},{4,20},{20... | collective-permute-start | bytes 7077896 | tf_op jit(solution)/shard_map/ppermute | solution.py:705
  194.7 16.7 %collective-permute-start.11 = (bf16[9216,128]{1,0:T(8,128)(2,1)}, bf16[9216,128]{1,0:T(8,128)(2,1)}, u32[]{:S(2)}, u32[]{:S(2)}) collective-permute-start(bf16[9216,128]{1,0:T(8,128)(2,1)} %get-tuple-element.129), channel_id=1, source_target_pairs={{0,16},{16,0},{1,17},{17,1},{2,18},{18,2},{3,19},{19,3},{4,20},{20... | collective-permute-start | bytes 7077896 | tf_op jit(solution)/shard_map/ppermute | solution.py:705
  218.0 59.2 %all-to-all-start.3 = ((bf16[16,144,384]{2,1,0:T(8,128)(2,1)}), bf16[16,144,384]{2,1,0:T(8,128)(2,1)S(1)}, u32[]{:S(2)}, u32[]{:S(2)}) async-start(bf16[16,144,384]{2,1,0:T(8,128)(2,1)} %shard_map.297), calls=%async_computation.3 | async-start | bytes 3538944 | tf_op jit(solution)/shard_map/all_to_all | solution.py:700
  278.4 58.7 %all-to-all-start.4 = ((bf16[16,144,384]{2,1,0:T(8,128)(2,1)}), bf16[16,144,384]{2,1,0:T(8,128)(2,1)S(1)}, u32[]{:S(2)}, u32[]{:S(2)}) async-start(bf16[16,144,384]{2,1,0:T(8,128)(2,1)} %constant_dynamic-update-slice_fusion.1), calls=%async_computation.4 | async-start | bytes 3538944 | tf_op jit(solution)/shard_map/all_to_all | solution.py:700
  337.1 45.7 %all-to-all-start.5 = ((bf16[16,144,384]{2,1,0:T(8,128)(2,1)}), bf16[16,144,384]{2,1,0:T(8,128)(2,1)}, u32[]{:S(2)}, u32[]{:S(2)}) async-start(bf16[16,144,384]{2,1,0:T(8,128)(2,1)} %constant_dynamic-update-slice_fusion), calls=%async_computation.5 | async-start | bytes 3538944 | tf_op jit(solution)/shard_map/all_to_all | solution.py:700
  344.0 219.8 %reduce-scatter.4.cloned.1.call-start = ((), (), s32[]{:S(2)}) async-start(), calls=%async_computation.10 | async-start | bytes 5898240
  375.4 50.3 %collective-permute-start.21 = (bf16[4,2,384,768]{3,2,1,0:T(8,128)(2,1)}, bf16[4,2,384,768]{3,2,1,0:T(8,128)(2,1)}, u32[]{:S(2)}, u32[]{:S(2)}) collective-permute-start(bf16[4,2,384,768]{3,2,1,0:T(8,128)(2,1)} %get-tuple-element.175), channel_id=1, source_target_pairs={{0,16},{16,0},{1,17},{17,1},{2,18},{18,2},{3,19},{19,3},{4,20},{20... | collective-permute-start | bytes 14155784 | tf_op jit(solution)/shard_map/ppermute | solution.py:705
  432.5 71.6 %all-to-all-start.6 = ((bf16[16,144,384]{2,1,0:T(8,128)(2,1)}), bf16[16,144,384]{2,1,0:T(8,128)(2,1)S(1)}, u32[]{:S(2)}, u32[]{:S(2)}) async-start(bf16[16,144,384]{2,1,0:T(8,128)(2,1)} %copy-done.37), calls=%async_computation.6 | async-start | bytes 3538944 | tf_op jit(solution)/shard_map/all_to_all | solution.py:700
  470.2 27.1 %collective-permute-start.19 = (bf16[9216,128]{1,0:T(8,128)(2,1)}, bf16[9216,128]{1,0:T(8,128)(2,1)}, u32[]{:S(2)}, u32[]{:S(2)}) collective-permute-start(bf16[9216,128]{1,0:T(8,128)(2,1)} %get-tuple-element.170), channel_id=1, source_target_pairs={{0,16},{16,0},{1,17},{17,1},{2,18},{18,2},{3,19},{19,3},{4,20},{20... | collective-permute-start | bytes 7077896 | tf_op jit(solution)/shard_map/ppermute | solution.py:705
  492.3 18.0 %collective-permute-start.34 = (f32[2,200,128]{2,1,0:T(8,128)}, f32[2,200,128]{2,1,0:T(8,128)}, u32[]{:S(2)}, u32[]{:S(2)}) collective-permute-start(f32[2,200,128]{2,1,0:T(8,128)} %pad_maximum_fusion.5), channel_id=1, source_target_pairs={{0,2},{1,3},{2,0},{3,1},{4,6},{5,7},{6,4},{7,5},{8,10},{9,11},{10,... | collective-permute-start | bytes 614408 | tf_op jit(solution)/shard_map/ppermute | solution.py:705
  504.7 56.7 %all-to-all-start.7 = ((bf16[16,144,384]{2,1,0:T(8,128)(2,1)}), bf16[16,144,384]{2,1,0:T(8,128)(2,1)}, u32[]{:S(2)}, u32[]{:S(2)}) async-start(bf16[16,144,384]{2,1,0:T(8,128)(2,1)} %copy-done.36), calls=%async_computation.7 | async-start | bytes 3538944 | tf_op jit(solution)/shard_map/all_to_all | solution.py:700
  511.3 16.7 %collective-permute-start.35 = (f32[4,200,128]{2,1,0:T(8,128)S(1)}, f32[4,200,128]{2,1,0:T(8,128)S(1)}, u32[]{:S(2)}, u32[]{:S(2)}) collective-permute-start(f32[4,200,128]{2,1,0:T(8,128)S(1)} %pad_maximum_fusion.4), channel_id=1, source_target_pairs={{0,4},{4,0},{8,12},{12,8},{1,5},{5,1},{9,13},{13,9},{2,6},{6,2},{1... | collective-permute-start | bytes 1228808 | tf_op jit(solution)/shard_map/ppermute | solution.py:705
  563.6 33.2 %collective-permute-start.27 = (bf16[8,144,384]{2,1,0:T(8,128)(2,1)}, bf16[8,144,384]{2,1,0:T(8,128)(2,1)}, u32[]{:S(2)}, u32[]{:S(2)}) collective-permute-start(bf16[8,144,384]{2,1,0:T(8,128)(2,1)} %constant_dynamic-slice_fusion.2), channel_id=1, source_target_pairs={{0,16},{16,0},{1,17},{17,1},{2,18},{18,2},{3,19},{19,3},{4,20},{20... | collective-permute-start | bytes 2654216 | tf_op jit(solution)/shard_map/ppermute | solution.py:705
  565.2 22.8 %collective-permute-start.23 = (bf16[2,96,768]{2,1,0:T(8,128)(2,1)S(1)}, bf16[2,96,768]{2,1,0:T(8,128)(2,1)S(1)}, u32[]{:S(2)}, u32[]{:S(2)}) collective-permute-start(bf16[2,96,768]{2,1,0:T(8,128)(2,1)S(1)} %get-tuple-element.262), channel_id=1, source_target_pairs={{0,2},{1,3},{2,0},{3,1},{4,6},{5,7},{6,4},{7,5},{8,10},{9,11},{10,... | collective-permute-start | bytes 884744 | tf_op jit(solution)/shard_map/ppermute | solution.py:705
  568.0 26.9 %collective-permute-start.24 = (bf16[2,96,768]{2,1,0:T(8,128)(2,1)S(1)}, bf16[2,96,768]{2,1,0:T(8,128)(2,1)S(1)}, u32[]{:S(2)}, u32[]{:S(2)}) collective-permute-start(bf16[2,96,768]{2,1,0:T(8,128)(2,1)S(1)} %get-tuple-element.261), channel_id=1, source_target_pairs={{0,3},{1,2},{2,1},{3,0},{4,7},{5,6},{6,5},{7,4},{8,11},{9,10},{10,... | collective-permute-start | bytes 884744 | tf_op jit(solution)/shard_map/ppermute | solution.py:705
  (104 other events, 1488.6 us)
Sparse Core Ops, SparseCore 0:
  65.8 86.3 all-gather.2
  432.2 79.4 reduce-scatter.3

commit v3 on v2

--- a/solution.py
+++ b/solution.py
@@ -636,14 +636,21 @@
     )(meta, frames, cot, recv, other, *consts, *kept)
 
 
-def weight_kernel(near, second_ref, branch_grad_ref, hid_ref, pre_grad_ref, own_ref, other_ref):
+def weight_kernel(near, second_ref, branch_grad_ref, hid_ref, pre_grad_ref, own_ref, *other_refs):
+    step = pl.program_id(0)
     sums = [dot_tn(pre_grad_ref[...], second_ref[...]), dot_tn(hid_ref[...], branch_grad_ref[...])]
-    for ref, mine in ((own_ref, pl.program_id(0) < near), (other_ref, pl.program_id(0) >= near)):
-
-        @pl.when(mine)
+
+    @pl.when(step < near)
+    def _():
+        for n in range(2):
+            own_ref[0, n] = sums[n].astype(bf16)
+
+    for m, ref in enumerate(other_refs):
+
+        @pl.when(step == near + m)
         def _():
             for n in range(2):
-                ref[0, n] = sums[n].astype(bf16)
+                ref[n] = sums[n].astype(bf16)
 
 
 def weight_call(kept, block):
@@ -651,16 +658,14 @@
     tokens, channels = second.shape
     wide = pl.BlockSpec((tokens, block), lambda n: (0, n))
     near = hid.shape[1] // block // 2
-    shape = (1, 2, block, channels)
+    shape = (2, block, channels)
     return pl.pallas_call(
         functools.partial(weight_kernel, near),
         grid=(2 * near,),
         in_specs=[full(second.shape), full(second.shape), wide, wide],
-        out_specs=[
-            pl.BlockSpec(shape, lambda n: (jnp.minimum(n, near - 1), 0, 0, 0)),
-            pl.BlockSpec(shape, lambda n: (jnp.maximum(n - near, 0), 0, 0, 0)),
-        ],
-        out_shape=[jax.ShapeDtypeStruct((near,) + shape[1:], bf16)] * 2,
+        out_specs=[pl.BlockSpec((1,) + shape, lambda n: (jnp.minimum(n, near - 1), 0, 0, 0))]
+        + [full(shape)] * near,
+        out_shape=[jax.ShapeDtypeStruct((near,) + shape, bf16)] + [jax.ShapeDtypeStruct(shape, bf16)] * near,
         compiler_params=params(48),
         cost_estimate=cost(22e9, 46e6),
     )(second, branch_grad, hid, pre_grad)
@@ -906,6 +911,15 @@
     parts = weight_call((queue(kept[0]),) + kept[1:], block)
     ran(parts[0])
     pair = start_waves(0, after(grads[0], *done))
+    if dp == 2 and parts[0].shape[0] == lon:
+        terms = [parts[0], jnp.stack([swap(v, "dp", 1) for v in parts[1:]])]
+    else:
+        parts = jnp.concatenate([parts[0], jnp.stack(parts[1:])], axis=0).transpose(1, 0, 2, 3)
+        parts = parts.reshape(2, dp, lon, lat * hidden_rows, channels).transpose(1, 2, 0, 3, 4)
+        terms = [parts[0]] + [swap(parts[n], "dp", n) for n in range(1, dp)]
+    own_part = add(terms).astype(bf16)
+    own_part, ahead = lax.optimization_barrier((own_part, pair[0]))
+    pair = (ahead, pair[1])
     for s in slots:
         pair, waves = waves_of(*pair, backward_middle, kept_waves[s], (), True)
         wave_sums.append(waves)
@@ -914,13 +928,6 @@
         field_sums.append(sums)
         sends.append(send)
         pair = following
-    if dp == 2 and parts[0].shape[0] == lon:
-        terms = [parts[0], after(swap(parts[1], "dp", 1), sends[0])]
-    else:
-        parts = jnp.concatenate(parts, axis=0).transpose(1, 0, 2, 3)
-        parts = parts.reshape(2, dp, lon, lat * hidden_rows, channels).transpose(1, 2, 0, 3, 4)
-        terms = [parts[0]] + [swap(parts[n], "dp", n) for n in range(1, dp)]
-    own_part = add(terms).astype(bf16)
     lat_part = lax.psum_scatter(own_part.reshape(lon, -1, channels), "lon", scatter_dimension=0)
     lat_part = lat_part.reshape(2, lat, hidden_rows, channels)
     ffn_grads = add([lat_part[:, 0]] + [swap(lat_part[:, n], "lat", n) for n in range(1, lat)])
@@ -948,7 +955,7 @@
     some_sums = all_sums
     all_sums = collect(all_sums, "lat", [1 << n for n in range(lat.bit_length() - 1)])
     all_sums = collect(all_sums, "lon", [1 << n for n in range(lon_blocks.bit_length() - 1)])
-    all_sums = collect(all_sums[None], "dp", [1])
+    all_sums = collect(after(all_sums[None], ffn_grads), "dp", [1])
     all_sums = jnp.concatenate([all_sums[0], all_sums[1]], axis=1)
     all_sums = all_sums[:, :, :size]
     inner_grad = all_sums[:, : 2 * size].reshape(blocks, 2, size, size)
@@ -962,8 +969,6 @@
         last = s + 1 == micro
         back.append(exchange(after(sends[s], *done, *((some_sums,) if last else ()))))
         done = (back[-1],)
-        if last:
-            ran(ffn_grads)
         frame_grads.append(
             last_call(plan, s, queue(metas[s]), frame_tiles, back[s], other(back[s]), grad_mixed[s], row(first_gain))
         )

time: 625 us -> 655 us (1.048)
  the two profiles are of different devices: /device:TPU:10 before, /device:TPU:0 now
where the time goes in v3:
time: 655 us; the launch traced here: 644 us
  Pallas kernels  242 us (37%)
  waiting for transfers between devices  189 us (29%)
  local copies, waits for them, and re-layouts  90.5 us (14%)
  starting transfers between devices  74.9 us (11%)
  other arithmetic  32.7 us (5%)
  between operations  15.4 us (2%)
    ppermute x40, waiting for transfers between devices, swap(): return lax.ppermute(value, axis, [(n, n ^ bit) for n in range(count)])  113 us
    pallas_call x2, Pallas kernels, ffn_call(): pl.pallas_call(functools.partial(ffn_kernel, plan, hidden, len(kept)), gr...  85.7 us
    all_to_all x8, waiting for transfers between devices, exchange(): return lax.all_to_all(values, ('lon', 'lat'), 0, 0, tiled=True)  75.9 us
    pallas_call x4, Pallas kernels, wave_call(): pl.pallas_call(functools.partial(wave_kernel, plan, middle, (len(streams_...  69.8 us
    unnamed x161, local copies, waits for them, and re-layouts  53.7 us
    all_to_all x8, starting transfers between devices, exchange(): return lax.all_to_all(values, ('lon', 'lat'), 0, 0, tiled=True)  47.8 us
    pallas_call x1, Pallas kernels, weight_call(): pl.pallas_call(functools.partial(weight_kernel, near), grid=(2 * near,),...  31.5 us
    ppermute x40, starting transfers between devices, swap(): return lax.ppermute(value, axis, [(n, n ^ bit) for n in range(count)])  26.8 us
  transfers between devices with their start and end apart: 50, of which 17 were waited for; matrix products, arithmetic and copies ran while one was open for 12% of the time, Pallas kernels for 35%

profile of v3, /device:TPU:0, one launch (start us, length us, event | category | flops | bytes accessed | tf_op | source)
XLA Modules:
  0.0 644.2 jit_solution(3029469076350876955)
XLA Ops:
  24.0 11.8 %collective-permute-done.2 = bf16[200,768]{1,0:T(8,128)(2,1)} collective-permute-done((bf16[200,768]{1,0:T(8,128)(2,1)}, bf16[200,768]{1,0:T(8,128)(2,1)}, u32[]{:S(2)}, u32[]{:S(2)}) %collective-permute-start.2) | collective-permute-done | bytes 307232 | tf_op jit(solution)/shard_map/ppermute | solution.py:710
  35.8 10.1 %collective-permute-done.3 = bf16[200,768]{1,0:T(8,128)(2,1)} collective-permute-done((bf16[200,768]{1,0:T(8,128)(2,1)}, bf16[200,768]{1,0:T(8,128)(2,1)}, u32[]{:S(2)}, u32[]{:S(2)}) %collective-permute-start.3) | collective-permute-done | bytes 307232 | tf_op jit(solution)/shard_map/ppermute | solution.py:710
  50.6 10.8 %all-to-all-start = ((bf16[16,144,384]{2,1,0:T(8,128)(2,1)}), bf16[16,144,384]{2,1,0:T(8,128)(2,1)}, u32[]{:S(2)}, u32[]{:S(2)}) async-start(bf16[16,144,384]{2,1,0:T(8,128)(2,1)} %constant_dynamic-update-slice_fusion.3), calls=%async_computation | async-start | bytes 3538944 | tf_op jit(solution)/shard_map/all_to_all | solution.py:705
  70.3 33.5 %all-to-all-done.recv_ref.refs_0_ = bf16[16,144,384]{2,1,0:T(8,128)(2,1)} async-done(((bf16[16,144,384]{2,1,0:T(8,128)(2,1)}), bf16[16,144,384]{2,1,0:T(8,128)(2,1)}, u32[]{:S(2)}, u32[]{:S(2)}) %all-to-all-start) | async-done | bytes 1769504 | tf_op jit(solution)/shard_map/all_to_all | solution.py:705
  103.9 6.0 shard_map.292
  119.3 16.8 %shard_map.293 = (bf16[9216,128]{1,0:T(8,128)(2,1)}, bf16[9216,128]{1,0:T(8,128)(2,1)}, bf16[8640,256]{1,0:T(8,128)(2,1)}, bf16[8640,256]{1,0:T(8,128)(2,1)}, bf16[8640,256]{1,0:T(8,128)(2,1)}) custom-call(bf16[2,4320,128]{2,1,0:T(8,128)(2,1)S(1)} %copy-done.31, bf16[2,4320,128]{2,1,0:T(8,128)(2,1)} %collective-permute-done.5.refs_1_, ...), custom_call_target="tpu_custom_call" | custom-call | flops 1000000000 | bytes 1200000 | tf_op jit(solution)/shard_map/pallas_call | solution.py:370
  145.8 16.7 %all-to-all-done.1.recv_ref.refs_0_ = bf16[16,144,384]{2,1,0:T(8,128)(2,1)S(1)} async-done(((bf16[16,144,384]{2,1,0:T(8,128)(2,1)}), bf16[16,144,384]{2,1,0:T(8,128)(2,1)S(1)}, u32[]{:S(2)}, u32[]{:S(2)}) %all-to-all-start.1) | async-done | bytes 1769504 | tf_op jit(solution)/shard_map/all_to_all | solution.py:705
  173.6 5.2 fusion.12
  179.4 16.8 %shard_map.296 = (bf16[9216,128]{1,0:T(8,128)(2,1)}, bf16[9216,128]{1,0:T(8,128)(2,1)}, bf16[8640,256]{1,0:T(8,128)(2,1)}, bf16[8640,256]{1,0:T(8,128)(2,1)}, bf16[8640,256]{1,0:T(8,128)(2,1)}) custom-call(bf16[2,4320,128]{2,1,0:T(8,128)(2,1)S(1)} %copy-done.33, bf16[2,4320,128]{2,1,0:T(8,128)(2,1)} %collective-permute-done.7.refs_1_, ...), custom_call_target="tpu_custom_call" | custom-call | flops 1000000000 | bytes 1200000 | tf_op jit(solution)/shard_map/pallas_call | solution.py:370
  203.1 15.0 %all-to-all-done.2.refs_3_ = bf16[16,144,384]{2,1,0:T(8,128)(2,1)} async-done(((bf16[16,144,384]{2,1,0:T(8,128)(2,1)}), bf16[16,144,384]{2,1,0:T(8,128)(2,1)}, u32[]{:S(2)}, u32[]{:S(2)}) %all-to-all-start.2) | async-done | bytes 1769504 | tf_op jit(solution)/shard_map/all_to_all | solution.py:705
  232.2 42.9 %shard_map.298 = (bf16[2304,768]{1,0:T(8,128)(2,1)}, bf16[2304,768]{1,0:T(8,128)(2,1)}, bf16[2304,3072]{1,0:T(8,128)(2,1)}, bf16[2304,3072]{1,0:T(8,128)(2,1)}, ...) custom-call(s32[7]{0:T(128)} %copy-done.47, ...), custom_call_target="tpu_custom_call" | custom-call | flops 2249999872 | bytes 3000000 | tf_op jit(solution)/shard_map/pallas_call | solution.py:613
  280.0 7.3 %all-to-all-start.4 = ((bf16[16,144,384]{2,1,0:T(8,128)(2,1)}), bf16[16,144,384]{2,1,0:T(8,128)(2,1)S(1)}, u32[]{:S(2)}, u32[]{:S(2)}) async-start(bf16[16,144,384]{2,1,0:T(8,128)(2,1)} %constant_dynamic-update-slice_fusion.1), calls=%async_computation.4 | async-start | bytes 3538944 | tf_op jit(solution)/shard_map/all_to_all | solution.py:705
  292.0 42.8 %shard_map.299 = (bf16[2304,768]{1,0:T(8,128)(2,1)}, bf16[2304,768]{1,0:T(8,128)(2,1)}, bf16[2304,3072]{1,0:T(8,128)(2,1)}, bf16[2304,3072]{1,0:T(8,128)(2,1)}, ...) custom-call(s32[7]{0:T(128)} %copy-done.49, ...), custom_call_target="tpu_custom_call", output_to_operand_aliasing={{0}: (15, {}), {1}: (16, {}), {2}: (17, {}), {3}: (18, {})} | custom-call | flops 2249999872 | bytes 3000000 | tf_op jit(solution)/shard_map/pallas_call | solution.py:613
  338.5 7.0 %all-to-all-start.5 = ((bf16[16,144,384]{2,1,0:T(8,128)(2,1)}), bf16[16,144,384]{2,1,0:T(8,128)(2,1)}, u32[]{:S(2)}, u32[]{:S(2)}) async-start(bf16[16,144,384]{2,1,0:T(8,128)(2,1)} %constant_dynamic-update-slice_fusion), calls=%async_computation.5 | async-start | bytes 3538944 | tf_op jit(solution)/shard_map/all_to_all | solution.py:705
  345.8 31.5 %shard_map.300 = (bf16[4,2,384,768]{3,2,1,0:T(8,128)(2,1)}, bf16[2,384,768]{2,1,0:T(8,128)(2,1)}, bf16[2,384,768]{2,1,0:T(8,128)(2,1)}, bf16[2,384,768]{2,1,0:T(8,128)(2,1)}, bf16[2,384,768]{2,1,0:T(8,128)(2,1)}) custom-call(bf16[2304,768]{1,0:T(8,128)(2,1)} %get-tuple-element.152.second_ref, bf16[2304,768]{1,0:T(8,128)(2,1)} %get-tuple-element.153.branch_grad_ref, ...), custom_call_target="tpu_custom_call" | custom-call | flops 1100000000 | bytes 2300000 | tf_op jit(solution)/shard_map/pallas_call | solution.py:662
  378.3 10.6 %all-to-all-done.5.recv_ref = bf16[16,144,384]{2,1,0:T(8,128)(2,1)} async-done(((bf16[16,144,384]{2,1,0:T(8,128)(2,1)}), bf16[16,144,384]{2,1,0:T(8,128)(2,1)}, u32[]{:S(2)}, u32[]{:S(2)}) %all-to-all-start.5) | async-done | bytes 1769504 | tf_op jit(solution)/shard_map/all_to_all | solution.py:705
  394.9 7.6 %add_convert_fusion = bf16[4,2,384,768]{3,2,1,0:T(8,128)(2,1)} fusion(bf16[4,2,384,768]{3,2,1,0:T(8,128)(2,1)} %get-tuple-element.156, bf16[1,2,384,768]{3,2,1,0:T(8,128)(2,1)} %bitcast.31, bf16[1,2,384,768]{3,2,1,0:T(8,128)(2,1)} %bitcast.30, bf16[1,2,384,768]{3,2,1,0:T(8,128)(2,1)} %bitcast.29, bf16[1,2,384,768]{3,2,1,0:T(8,128)(2,1)} %bitcast.28), kind=kLoop, calls=%fused_computation | loop fusion | flops 16515072 | bytes 14155776 | tf_op jit(solution)/shard_map/convert_element_type | solution.py:920
  405.3 18.3 %shard_map.302 = (bf16[9216,128]{1,0:T(8,128)(2,1)}, bf16[9216,128]{1,0:T(8,128)(2,1)}, f32[400,128]{1,0:T(8,128)S(1)}) custom-call(bf16[2,4320,128]{2,1,0:T(8,128)(2,1)S(1)} %copy-done.37, bf16[2,4320,128]{2,1,0:T(8,128)(2,1)} %collective-permute-done.20.refs_1_, bf16[192,192]{1,0:T(8,128)(2,1)S(1)} %copy-done.24, bf16[192,192]{1,0:T(8,128)(2,1)S(1)} %copy-done.21, ...), custom_call_target="tpu_custom_call" | custom-call | flops 1000000000 | bytes 1200000 | tf_op jit(solution)/shard_map/pallas_call | solution.py:370
  423.6 6.1 shard_map.303
  455.6 17.9 %shard_map.305 = (bf16[9216,128]{1,0:T(8,128)(2,1)}, bf16[9216,128]{1,0:T(8,128)(2,1)}, f32[400,128]{1,0:T(8,128)S(1)}) custom-call(bf16[2,4320,128]{2,1,0:T(8,128)(2,1)S(1)} %copy-done.35, bf16[2,4320,128]{2,1,0:T(8,128)(2,1)} %collective-permute-done.22.refs_1_, bf16[192,192]{1,0:T(8,128)(2,1)S(1)} %copy-done.25, bf16[192,192]{1,0:T(8,128)(2,1)S(1)} %copy-done.22, ...), custom_call_target="tpu_custom_call" | custom-call | flops 1000000000 | bytes 1200000 | tf_op jit(solution)/shard_map/pallas_call | solution.py:370
  505.6 6.8 %all-to-all-start.7 = ((bf16[16,144,384]{2,1,0:T(8,128)(2,1)}), bf16[16,144,384]{2,1,0:T(8,128)(2,1)}, u32[]{:S(2)}, u32[]{:S(2)}) async-start(bf16[16,144,384]{2,1,0:T(8,128)(2,1)} %copy-done.38), calls=%async_computation.7 | async-start | bytes 3538944 | tf_op jit(solution)/shard_map/all_to_all | solution.py:705
  516.8 43.8 %collective-permute-done.34 = f32[2,200,128]{2,1,0:T(8,128)S(1)} collective-permute-done((f32[2,200,128]{2,1,0:T(8,128)S(1)}, f32[2,200,128]{2,1,0:T(8,128)S(1)}, u32[]{:S(2)}, u32[]{:S(2)}) %collective-permute-start.34) | collective-permute-done | bytes 204832 | tf_op jit(solution)/shard_map/ppermute | solution.py:710
  584.2 24.3 %collective-permute-done.32 = f32[66,128]{1,0:T(8,128)S(1)} collective-permute-done((f32[66,128]{1,0:T(8,128)S(1)}, f32[66,128]{1,0:T(8,128)S(1)}, u32[]{:S(2)}, u32[]{:S(2)}) %collective-permute-start.32) | collective-permute-done | bytes 33824 | tf_op jit(solution)/shard_map/ppermute | solution.py:710
  627.4 5.2 shard_map.308
  (351 shorter events, 214.0 us)
Async XLA Ops:
  18.4 30.0 %collective-permute-start = (bf16[8,144,384]{2,1,0:T(8,128)(2,1)}, bf16[8,144,384]{2,1,0:T(8,128)(2,1)}, u32[]{:S(2)}, u32[]{:S(2)}) collective-permute-start(bf16[8,144,384]{2,1,0:T(8,128)(2,1)} %get-tuple-element.114), channel_id=1, source_target_pairs={{0,16},{16,0},{1,17},{17,1},{2,18},{18,2},{3,19},{19,3},{4,20},{20... | collective-permute-start | bytes 2654216 | tf_op jit(solution)/shard_map/ppermute | solution.py:710
  21.4 24.5 %collective-permute-start.3 = (bf16[200,768]{1,0:T(8,128)(2,1)}, bf16[200,768]{1,0:T(8,128)(2,1)}, u32[]{:S(2)}, u32[]{:S(2)}) collective-permute-start(bf16[200,768]{1,0:T(8,128)(2,1)} %get-tuple-element.290), channel_id=1, source_target_pairs={{0,2},{1,3},{2,0},{3,1},{4,6},{5,7},{6,4},{7,5},{8,10},{9,11},{10,... | collective-permute-start | bytes 921608 | tf_op jit(solution)/shard_map/ppermute | solution.py:710
  24.0 21.9 %collective-permute-start.4 = (bf16[200,768]{1,0:T(8,128)(2,1)}, bf16[200,768]{1,0:T(8,128)(2,1)}, u32[]{:S(2)}, u32[]{:S(2)}) collective-permute-start(bf16[200,768]{1,0:T(8,128)(2,1)} %get-tuple-element.290), channel_id=1, source_target_pairs={{0,3},{1,2},{2,1},{3,0},{4,7},{5,6},{6,5},{7,4},{8,11},{9,10},{10,... | collective-permute-start | bytes 921608 | tf_op jit(solution)/shard_map/ppermute | solution.py:710
  50.6 53.3 %all-to-all-start = ((bf16[16,144,384]{2,1,0:T(8,128)(2,1)}), bf16[16,144,384]{2,1,0:T(8,128)(2,1)}, u32[]{:S(2)}, u32[]{:S(2)}) async-start(bf16[16,144,384]{2,1,0:T(8,128)(2,1)} %constant_dynamic-update-slice_fusion.3), calls=%async_computation | async-start | bytes 3538944 | tf_op jit(solution)/shard_map/all_to_all | solution.py:705
  61.3 112.3 %all-gather.3.cloned.1.call-start = ((), (), s32[]{:S(2)}) async-start(), calls=%async_computation.9 | async-start | bytes 6144000 | tf_op jit(solution)/shard_map/all_gather | solution.py:820
  112.0 50.5 %all-to-all-start.1 = ((bf16[16,144,384]{2,1,0:T(8,128)(2,1)}), bf16[16,144,384]{2,1,0:T(8,128)(2,1)S(1)}, u32[]{:S(2)}, u32[]{:S(2)}) async-start(bf16[16,144,384]{2,1,0:T(8,128)(2,1)} %constant_dynamic-update-slice_fusion.2), calls=%async_computation.1 | async-start | bytes 3538944 | tf_op jit(solution)/shard_map/all_to_all | solution.py:705
  168.9 49.1 %all-to-all-start.2 = ((bf16[16,144,384]{2,1,0:T(8,128)(2,1)}), bf16[16,144,384]{2,1,0:T(8,128)(2,1)}, u32[]{:S(2)}, u32[]{:S(2)}) async-start(bf16[16,144,384]{2,1,0:T(8,128)(2,1)} %shard_map.294), calls=%async_computation.2 | async-start | bytes 3538944 | tf_op jit(solution)/shard_map/all_to_all | solution.py:705
  178.8 24.3 %collective-permute-start.10 = (bf16[1536,768]{1,0:T(8,128)(2,1)}, bf16[1536,768]{1,0:T(8,128)(2,1)}, u32[]{:S(2)}, u32[]{:S(2)}) collective-permute-start(bf16[1536,768]{1,0:T(8,128)(2,1)} %bitcast.25.refs_13_), channel_id=1, source_target_pairs={{0,16},{16,0},{1,17},{17,1},{2,18},{18,2},{3,19},{19,3},{4,20},{20... | collective-permute-start | bytes 7077896 | tf_op jit(solution)/shard_map/ppermute | solution.py:710
  179.3 23.8 %collective-permute-start.9 = (bf16[1536,768]{1,0:T(8,128)(2,1)}, bf16[1536,768]{1,0:T(8,128)(2,1)}, u32[]{:S(2)}, u32[]{:S(2)}) collective-permute-start(bf16[1536,768]{1,0:T(8,128)(2,1)} %bitcast.24.refs_11_), channel_id=1, source_target_pairs={{0,16},{16,0},{1,17},{17,1},{2,18},{18,2},{3,19},{19,3},{4,20},{20... | collective-permute-start | bytes 7077896 | tf_op jit(solution)/shard_map/ppermute | solution.py:710
  196.1 21.9 %collective-permute-start.11 = (bf16[9216,128]{1,0:T(8,128)(2,1)}, bf16[9216,128]{1,0:T(8,128)(2,1)}, u32[]{:S(2)}, u32[]{:S(2)}) collective-permute-start(bf16[9216,128]{1,0:T(8,128)(2,1)} %get-tuple-element.135), channel_id=1, source_target_pairs={{0,16},{16,0},{1,17},{17,1},{2,18},{18,2},{3,19},{19,3},{4,20},{20... | collective-permute-start | bytes 7077896 | tf_op jit(solution)/shard_map/ppermute | solution.py:710
  224.6 54.2 %all-to-all-start.3 = ((bf16[16,144,384]{2,1,0:T(8,128)(2,1)}), bf16[16,144,384]{2,1,0:T(8,128)(2,1)S(1)}, u32[]{:S(2)}, u32[]{:S(2)}) async-start(bf16[16,144,384]{2,1,0:T(8,128)(2,1)} %shard_map.297), calls=%async_computation.3 | async-start | bytes 3538944 | tf_op jit(solution)/shard_map/all_to_all | solution.py:705
  280.0 58.5 %all-to-all-start.4 = ((bf16[16,144,384]{2,1,0:T(8,128)(2,1)}), bf16[16,144,384]{2,1,0:T(8,128)(2,1)S(1)}, u32[]{:S(2)}, u32[]{:S(2)}) async-start(bf16[16,144,384]{2,1,0:T(8,128)(2,1)} %constant_dynamic-update-slice_fusion.1), calls=%async_computation.4 | async-start | bytes 3538944 | tf_op jit(solution)/shard_map/all_to_all | solution.py:705
  338.5 50.4 %all-to-all-start.5 = ((bf16[16,144,384]{2,1,0:T(8,128)(2,1)}), bf16[16,144,384]{2,1,0:T(8,128)(2,1)}, u32[]{:S(2)}, u32[]{:S(2)}) async-start(bf16[16,144,384]{2,1,0:T(8,128)(2,1)} %constant_dynamic-update-slice_fusion), calls=%async_computation.5 | async-start | bytes 3538944 | tf_op jit(solution)/shard_map/all_to_all | solution.py:705
  345.6 229.0 %reduce-scatter.4.cloned.1.call-start = ((), (), s32[]{:S(2)}) async-start(), calls=%async_computation.10 | async-start | bytes 5898240
  438.4 67.2 %all-to-all-start.6 = ((bf16[16,144,384]{2,1,0:T(8,128)(2,1)}), bf16[16,144,384]{2,1,0:T(8,128)(2,1)S(1)}, u32[]{:S(2)}, u32[]{:S(2)}) async-start(bf16[16,144,384]{2,1,0:T(8,128)(2,1)} %copy-done.39), calls=%async_computation.6 | async-start | bytes 3538944 | tf_op jit(solution)/shard_map/all_to_all | solution.py:705
  474.2 23.0 %collective-permute-start.23 = (bf16[9216,128]{1,0:T(8,128)(2,1)}, bf16[9216,128]{1,0:T(8,128)(2,1)}, u32[]{:S(2)}, u32[]{:S(2)}) collective-permute-start(bf16[9216,128]{1,0:T(8,128)(2,1)} %get-tuple-element.182), channel_id=1, source_target_pairs={{0,16},{16,0},{1,17},{17,1},{2,18},{18,2},{3,19},{19,3},{4,20},{20... | collective-permute-start | bytes 7077896 | tf_op jit(solution)/shard_map/ppermute | solution.py:710
  505.6 114.0 %all-to-all-start.7 = ((bf16[16,144,384]{2,1,0:T(8,128)(2,1)}), bf16[16,144,384]{2,1,0:T(8,128)(2,1)}, u32[]{:S(2)}, u32[]{:S(2)}) async-start(bf16[16,144,384]{2,1,0:T(8,128)(2,1)} %copy-done.38), calls=%async_computation.7 | async-start | bytes 3538944 | tf_op jit(solution)/shard_map/all_to_all | solution.py:705
  512.4 48.2 %collective-permute-start.34 = (f32[2,200,128]{2,1,0:T(8,128)S(1)}, f32[2,200,128]{2,1,0:T(8,128)S(1)}, u32[]{:S(2)}, u32[]{:S(2)}) collective-permute-start(f32[2,200,128]{2,1,0:T(8,128)S(1)} %pad_maximum_fusion.5), channel_id=1, source_target_pairs={{0,2},{1,3},{2,0},{3,1},{4,6},{5,7},{6,4},{7,5},{8,10},{9,11},{10,... | collective-permute-start | bytes 614408 | tf_op jit(solution)/shard_map/ppermute | solution.py:710
  516.7 44.0 %collective-permute-start.28 = (f32[66,128]{1,0:T(8,128)S(1)}, f32[66,128]{1,0:T(8,128)S(1)}, u32[]{:S(2)}, u32[]{:S(2)}) collective-permute-start(f32[66,128]{1,0:T(8,128)S(1)} %bitcast.126), channel_id=1, source_target_pairs={{0,16},{16,0},{1,17},{17,1},{2,18},{18,2},{3,19},{19,3},{4,20},{20... | collective-permute-start | bytes 101384 | tf_op jit(solution)/shard_map/ppermute | solution.py:710
  574.6 37.1 %collective-permute-start.24 = (bf16[8,144,384]{2,1,0:T(8,128)(2,1)}, bf16[8,144,384]{2,1,0:T(8,128)(2,1)}, u32[]{:S(2)}, u32[]{:S(2)}) collective-permute-start(bf16[8,144,384]{2,1,0:T(8,128)(2,1)} %constant_dynamic-slice_fusion.4), channel_id=1, source_target_pairs={{0,16},{16,0},{1,17},{17,1},{2,18},{18,2},{3,19},{19,3},{4,20},{20... | collective-permute-start | bytes 2654216 | tf_op jit(solution)/shard_map/ppermute | solution.py:710
  575.8 32.7 %collective-permute-start.36 = (bf16[2,96,768]{2,1,0:T(8,128)(2,1)S(1)}, bf16[2,96,768]{2,1,0:T(8,128)(2,1)S(1)}, u32[]{:S(2)}, u32[]{:S(2)}) collective-permute-start(bf16[2,96,768]{2,1,0:T(8,128)(2,1)S(1)} %get-tuple-element.272), channel_id=1, source_target_pairs={{0,1},{1,0},{2,3},{3,2},{4,5},{5,4},{6,7},{7,6},{8,9},{9,8},{10,11... | collective-permute-start | bytes 884744 | tf_op jit(solution)/shard_map/ppermute | solution.py:710
  577.9 30.6 %collective-permute-start.37 = (bf16[2,96,768]{2,1,0:T(8,128)(2,1)S(1)}, bf16[2,96,768]{2,1,0:T(8,128)(2,1)S(1)}, u32[]{:S(2)}, u32[]{:S(2)}) collective-permute-start(bf16[2,96,768]{2,1,0:T(8,128)(2,1)S(1)} %get-tuple-element.274), channel_id=1, source_target_pairs={{0,2},{1,3},{2,0},{3,1},{4,6},{5,7},{6,4},{7,5},{8,10},{9,11},{10,... | collective-permute-start | bytes 884744 | tf_op jit(solution)/shard_map/ppermute | solution.py:710
  578.7 29.8 %collective-permute-start.38 = (bf16[2,96,768]{2,1,0:T(8,128)(2,1)S(1)}, bf16[2,96,768]{2,1,0:T(8,128)(2,1)S(1)}, u32[]{:S(2)}, u32[]{:S(2)}) collective-permute-start(bf16[2,96,768]{2,1,0:T(8,128)(2,1)S(1)} %get-tuple-element.273), channel_id=1, source_target_pairs={{0,3},{1,2},{2,1},{3,0},{4,7},{5,6},{6,5},{7,4},{8,11},{9,10},{10,... | collective-permute-start | bytes 884744 | tf_op jit(solution)/shard_map/ppermute | solution.py:710
  581.4 27.1 %collective-permute-start.32 = (f32[66,128]{1,0:T(8,128)S(1)}, f32[66,128]{1,0:T(8,128)S(1)}, u32[]{:S(2)}, u32[]{:S(2)}) collective-permute-start(f32[66,128]{1,0:T(8,128)S(1)} %add.168), channel_id=1, source_target_pairs={{0,2},{1,3},{2,0},{3,1},{4,6},{5,7},{6,4},{7,5},{8,10},{9,11},{10,... | collective-permute-start | bytes 101384 | tf_op jit(solution)/shard_map/ppermute | solution.py:710
  (101 other events, 1496.1 us)
Sparse Core Ops, SparseCore 0:
  66.9 86.1 all-gather.2
  402.8 71.5 reduce-scatter.3
